TPU v7x, 512 devices: a whole 4x8x8 slice. The times are simulated.
512 devices in a mesh: ctx: 16 (over y, x_hi), head: 32 (over z, x_lo, core).
Axes of the slice: x: 4 (x_hi: 2, x_lo: 2; x = x_hi * 2 + x_lo), y: 8, z: 8, core: 2. Of those that a mesh axis runs over, the one named last changes fastest.
Arguments:
- queries: bfloat16 [512, 12288], P('ctx', 'head'), may hold values from -6 to 6
- cache_keys: bfloat16 [32, 16384, 128], P('head', 'ctx'), may hold values from -6 to 6
- cache_values: bfloat16 [32, 16384, 128], P('head', 'ctx'), may hold values from -6 to 6
- turn_keys: bfloat16 [32, 128, 128], P('head', 'ctx'), may hold values from -12 to 12
- turn_values: bfloat16 [32, 128, 128], P('head', 'ctx'), may hold values from -6 to 6
- cache_fill: int32 [16], P('ctx'), may hold values from 1 to 1024, 8192 in all
- turn_positions: int32 [512], replicated, may hold values from 0 to 511, each once
Outputs:
- attention_out: bfloat16 [512, 12288], P('ctx', 'head')
Inputs may be any that keep to these rules, and one draw needn't show every extreme that they name: `turn_positions`: each of 0 to 511 exactly once.
All inputs are finite; a program needn't handle non-finite values. No bound on the sum of `cache_fill` on one device may be relied on, other than what follows from the above.
Results may differ from a plain program's by a relative error of at most 0.005.
Values may be sent and summed in bfloat16 or wider, within the bound.
No kernel may reach another device: no remote copies, remote signals or barrier semaphores. Data moves between devices by JAX's collectives and lax.ppermute only.
A program may use at most 128 MiB of HBM per device.

v0:
```python
import math

import jax
import jax.numpy as jnp
from jax import lax
from jax.sharding import PartitionSpec as P

Q_HEADS = 96
KV_HEADS = 8


NEGATIVE = -1e30


def swapped(block, axis, bit):
    count = lax.axis_size(axis)
    route = []
    for low in range(count):
        high = low | 1 << bit
        if high != low and high < count:
            route += [(low, high), (high, low)]
    return lax.ppermute(block, axis, route)


def attend(block_q, keys, values, visible, scale):
    scores = jnp.einsum("tgd,kd->tgk", block_q, keys, preferred_element_type=jnp.float32) * scale
    masked = jnp.where(visible[:, None, :], scores, NEGATIVE)
    peak = jnp.max(masked, axis=2)
    weights = jnp.where(visible[:, None, :], jnp.exp(masked - peak[:, :, None]), 0.0)
    total = jnp.sum(weights, axis=2)
    mixed = jnp.einsum(
        "tgk,kd->tgd", weights.astype(jnp.bfloat16), values, preferred_element_type=jnp.float32
    )
    return (mixed, peak, total)


def combine(first, second):
    peak = jnp.maximum(first[1], second[1])
    left = jnp.exp(first[1] - peak)
    right = jnp.exp(second[1] - peak)
    mixed = first[0] * left[:, :, None] + second[0] * right[:, :, None]
    return (mixed, peak, first[2] * left + second[2] * right)


def body(queries, cache_keys, cache_values, turn_keys, turn_values, cache_fill, turn_positions):
    tok_rows = queries.shape[0]
    width = cache_keys.shape[2]
    own_heads = queries.shape[1] // width
    group = Q_HEADS // KV_HEADS
    scale = 1.0 / math.sqrt(width)
    ctx_count = lax.axis_size("ctx")
    parts = lax.axis_size("head") // KV_HEADS
    levels = parts.bit_length() - 1
    head_index = lax.axis_index("head")
    ctx_index = lax.axis_index("ctx")
    sub_index = head_index % parts
    all_tokens = tok_rows * ctx_count
    turn_dev = turn_keys.shape[1]
    gathered = queries
    for level in range(levels):
        partner = swapped(gathered, "head", level)
        upper = head_index // 2**level % 2
        gathered = jnp.where(
            upper == 1,
            jnp.concatenate([partner, gathered], axis=1),
            jnp.concatenate([gathered, partner], axis=1),
        )
    group_q = gathered.reshape(tok_rows, group, width)
    local_k = cache_keys[0]
    local_v = cache_values[0]
    slot_ok = jnp.arange(local_k.shape[0], dtype=jnp.int32) < cache_fill[0]
    fresh_k = turn_keys[0]
    fresh_v = turn_values[0]
    turn_base = sub_index * (all_tokens // parts)
    fresh_pos = lax.dynamic_slice_in_dim(turn_positions, turn_base + ctx_index * turn_dev, turn_dev)
    piece = lax.all_gather(group_q, "ctx", axis=0, tiled=True)
    count = piece.shape[0]
    seen = jnp.broadcast_to(slot_ok[None, :], (count, local_k.shape[0]))
    cached = attend(piece, local_k, local_v, seen, scale)
    fresh = attend(piece, fresh_k, fresh_v, fresh_pos[None, :] <= turn_positions[:, None], scale)
    merged = combine(cached, fresh)
    mixed, peak, total = tuple((new for new in merged))
    flat = mixed.reshape(all_tokens, group * width)
    got_mixed, got_peak, got_total = (
        lax.all_to_all(flat, "ctx", split_axis=0, concat_axis=1, tiled=True),
        lax.all_to_all(peak, "ctx", split_axis=0, concat_axis=1, tiled=True),
        lax.all_to_all(total, "ctx", split_axis=0, concat_axis=1, tiled=True),
    )
    got_mixed = got_mixed.reshape(tok_rows, ctx_count, group, width)
    got_peak = got_peak.reshape(tok_rows, ctx_count, group)
    got_total = got_total.reshape(tok_rows, ctx_count, group)
    best = jnp.max(got_peak, axis=1)
    factor = jnp.exp(got_peak - best[:, None, :])
    state = (
        jnp.sum(got_mixed * factor[:, :, :, None], axis=1),
        best,
        jnp.sum(got_total * factor, axis=1),
    )
    mixed, peak, total = state
    for level in reversed(range(levels)):
        half = mixed.shape[1] // 2
        keep_low = head_index // 2**level % 2 == 0
        low_part = (mixed[:, :half], peak[:, :half], total[:, :half])
        high_part = (mixed[:, half:], peak[:, half:], total[:, half:])
        mine = tuple((jnp.where(keep_low, low, high) for low, high in zip(low_part, high_part)))
        theirs = tuple((jnp.where(keep_low, high, low) for low, high in zip(low_part, high_part)))
        arrived = swapped(theirs, "head", level)
        mixed, peak, total = combine(mine, arrived)
    return (mixed / total[:, :, None]).reshape(tok_rows, own_heads * width).astype(jnp.bfloat16)


def solution(mesh):
    in_specs = (
        P("ctx", "head"),
        P("head", "ctx", None),
        P("head", "ctx", None),
        P("head", "ctx", None),
        P("head", "ctx", None),
        P("ctx"),
        P(),
    )
    out_specs = P("ctx", "head")
    return jax.shard_map(body, mesh=mesh, in_specs=in_specs, out_specs=out_specs, check_vma=False)
```

profile of v0, /device:TPU:1, one launch (start us, length us, event | category | flops | bytes accessed | tf_op | source)
XLA Modules:
  0.0 283.8 jit_solution(9354190547808743154)
XLA Ops:
  6.5 8.9 %collective-permute-start = (bf16[32,384]{1,0:T(8,128)(2,1)}, bf16[32,384]{1,0:T(8,128)(2,1)S(1)}, u32[]{:S(2)}, u32[]{:S(2)}) collective-permute-start(bf16[32,384]{1,0:T(8,128)(2,1)} %param.7), channel_id=1, source_target_pairs={{0,1},{1,0},{2,3},{3,2},{4,5},{5,4},{6,7},{7,6},{8,9},{9,8},{10,11... | collective-permute-start | bytes 73736 | tf_op jit(solution)/shard_map/ppermute | solution.py:22
  15.5 0.7 copy_bitcast_fusion.2
  16.2 0.3 collective-permute-done
  16.5 0.8 maximum_select_fusion.1
  17.3 1.9 collective-permute-start.1
  19.3 2.9 %collective-permute-done.1 = bf16[32,768]{1,0:T(8,128)(2,1)S(1)} collective-permute-done((bf16[32,768]{1,0:T(8,128)(2,1)S(1)}, bf16[32,768]{1,0:T(8,128)(2,1)S(1)}, u32[]{:S(2)}, u32[]{:S(2)}) %collective-permute-start.1) | collective-permute-done | bytes 49184 | tf_op jit(solution)/shard_map/ppermute | solution.py:22
  22.2 0.6 maximum_select_fusion
  23.5 0.8 dynamic_slice.3
  24.3 0.8 broadcast_compare_fusion
  25.0 79.9 %all-gather.2.cloned.1.call-done = bf16[512,12,128]{2,0,1:T(8,128)(2,1)} async-done(((bf16[32,12,128]{2,0,1:T(8,128)(2,1)}), bf16[512,12,128]{2,0,1:T(8,128)(2,1)}) %all-gather.2.cloned.1.call-update) | async-done | bytes 1572880 | tf_op jit(solution)/shard_map/all_gather | solution.py:76
  104.9 1.9 fusion.35
  106.9 0.7 reduce_max.34
  107.7 0.7 reduce_sum.47
  108.4 11.5 %fusion = (f32[512,12]{0,1:T(8,128)S(1)}, f32[512,12,1024]{2,0,1:T(8,128)}) fusion(pred[1024]{0:T(1024)(128)(4,1)S(1)} %iota_compare_fusion, bf16[512,12,128]{2,0,1:T(8,128)(2,1)} %all-gather.2.cloned.1.call-done, bf16[1,1024,128]{2,1,0:T(8,128)(2,1)S(1)} %copy-done), kind=kOutput, calls=%fused_computation.2 | convolution fusion | flops 1629480960 | bytes 27026432 | tf_op jit(solution)/shard_map/tgd,kd->tgk/dot_general | solution.py:26
  119.9 0.7 reduce_max.33
  120.7 11.7 %fusion.1 = f32[512,12]{0,1:T(8,128)S(1)} fusion(f32[512,12,1024]{2,0,1:T(8,128)} %get-tuple-element.19, f32[512,12]{0,1:T(8,128)S(1)} %get-tuple-element.18, pred[1024]{0:T(1024)(128)(4,1)S(1)} %iota_compare_fusion), kind=kLoop, calls=%fused_computation.3 | loop fusion | flops 31451136 | bytes 25216000 | tf_op jit(solution)/shard_map/reduce_sum | solution.py:30
  132.4 10.7 %fusion.3 = f32[512,12,128]{2,0,1:T(8,128)S(1)} fusion(f32[512,12,1024]{2,0,1:T(8,128)} %get-tuple-element.19, f32[512,12]{0,1:T(8,128)S(1)} %get-tuple-element.18, pred[1024]{0:T(1024)(128)(4,1)S(1)} %iota_compare_fusion, bf16[1,1024,128]{2,1,0:T(8,128)(2,1)S(1)} %copy-done.3), kind=kOutput, calls=%fused_computation.5 | convolution fusion | flops 1642070016 | bytes 28599296 | tf_op jit(solution)/shard_map/tgk,kd->tgd/dot_general | solution.py:31
  143.1 0.7 reduce_sum.45
  143.8 1.7 multiply_add_fusion.2
  145.5 0.7 copy.66
  146.2 1.6 reshape.87
  147.8 4.1 %all-to-all-start.2 = ((f32[16,1,384]{2,1,0:T(1,128)}), f32[16,1,384]{2,1,0:T(1,128)}, u32[]{:S(2)}, u32[]{:S(2)}) async-start(f32[16,1,384]{2,1,0:T(1,128)} %reshape.87), calls=%async_computation.2 | async-start | bytes 49152 | tf_op jit(solution)/shard_map/all_to_all | solution.py:87
  151.9 1.6 copy.67
  153.4 1.6 reshape.85
  155.1 5.8 %all-to-all-done.2 = f32[16,1,384]{2,1,0:T(1,128)} async-done(((f32[16,1,384]{2,1,0:T(1,128)}), f32[16,1,384]{2,1,0:T(1,128)}, u32[]{:S(2)}, u32[]{:S(2)}) %all-to-all-start.2) | async-done | bytes 24608 | tf_op jit(solution)/shard_map/all_to_all | solution.py:87
  160.8 3.5 %all-to-all-start.1 = ((f32[16,1,384]{2,1,0:T(1,128)}), f32[16,1,384]{2,1,0:T(1,128)S(1)}, u32[]{:S(2)}, u32[]{:S(2)}) async-start(f32[16,1,384]{2,1,0:T(1,128)} %reshape.85), calls=%async_computation.1 | async-start | bytes 49152 | tf_op jit(solution)/shard_map/all_to_all | solution.py:86
  164.3 3.4 %multiply_add_fusion = f32[512,12,128]{2,0,1:T(8,128)S(1)} fusion(f32[512,12,128]{2,0,1:T(8,128)S(1)} %fusion.3, f32[512,12]{0,1:T(8,128)S(1)} %get-tuple-element.17, f32[512,12]{0,1:T(8,128)S(1)} %get-tuple-element.16, f32[512,12,8]{0,2,1:T(8,128)} %copy-done.1, f32[512,12]{0,1:T(8,128)S(1)} %get-tuple-element.20, ...), kind=kOutput, calls=%fused_computation.9 | convolution fusion | flops 15089664 | bytes 6567936 | tf_op jit(solution)/shard_map/tgk,kd->tgd/dot_general | solution.py:31
  167.8 3.8 %copy.38 = f32[512,12,128]{2,1,0:T(8,128)} copy(f32[512,12,128]{2,0,1:T(8,128)S(1)} %multiply_add_fusion) | data formatting | bytes 6291456 | tf_op jit(solution)/shard_map/add | solution.py:41
  171.6 4.7 %all_to_all.32 = f32[16,32,1536]{2,1,0:T(8,128)} reshape(f32[512,12,128]{2,1,0:T(8,128)} %copy.38) | data formatting | bytes 6291456 | tf_op jit(solution)/shard_map/all_to_all | solution.py:85
  176.3 9.0 %all-to-all-start = ((f32[16,32,1536]{2,1,0:T(8,128)}), f32[16,32,1536]{2,1,0:T(8,128)}, u32[]{:S(2)}, u32[]{:S(2)}) async-start(f32[16,32,1536]{2,1,0:T(8,128)} %all_to_all.32), calls=%async_computation | async-start | bytes 6291456 | tf_op jit(solution)/shard_map/all_to_all | solution.py:85
  185.3 0.5 broadcast.36
  185.8 1.4 reduce.2
  187.4 0.7 reduce.1
  188.3 2.9 %collective-permute-start.2 = (f32[32,6]{0,1:T(8,128)S(1)}, f32[32,6]{0,1:T(8,128)S(1)}, u32[]{:S(2)}, u32[]{:S(2)}) collective-permute-start(f32[32,6]{0,1:T(8,128)S(1)} %slice_select_fusion.3), channel_id=1, source_target_pairs={{0,2},{2,0},{1,3},{3,1},{4,6},{6,4},{5,7},{7,5},{8,10},{10,8},{9,1... | collective-permute-start | bytes 2312 | tf_op jit(solution)/shard_map/ppermute | solution.py:22
  191.1 2.6 collective-permute-start.6
  193.8 0.2 copy.41
  194.0 2.6 mul.110
  196.5 3.0 %mul.111 = f32[32,16,1536]{2,1,0:T(8,128)S(1)} reshape(f32[32,16,12,128]{3,2,1,0:T(8,128)} %mul.110) | data formatting | bytes 6291456 | tf_op jit(solution)/shard_map/mul | solution.py:95
  199.6 56.8 %all-to-all-done = f32[16,32,1536]{2,1,0:T(8,128)} async-done(((f32[16,32,1536]{2,1,0:T(8,128)}), f32[16,32,1536]{2,1,0:T(8,128)}, u32[]{:S(2)}, u32[]{:S(2)}) %all-to-all-start) | async-done | bytes 3145760 | tf_op jit(solution)/shard_map/all_to_all | solution.py:85
  256.5 4.5 %fusion.6 = f32[32,1536]{1,0:T(8,128)} fusion(f32[16,32,1536]{2,1,0:T(8,128)} %all-to-all-done, f32[32,16,1536]{2,1,0:T(8,128)S(1)} %mul.111), kind=kLoop, calls=%fused_computation.8 | loop fusion | flops 1523712 | bytes 6488064 | tf_op jit(solution)/shard_map/reduce_sum | solution.py:95
  261.0 1.0 reduce_sum.43
  262.0 2.5 collective-permute-start.3
  264.5 6.1 %collective-permute-start.4 = (f32[32,3]{0,1:T(4,128)S(1)}, f32[32,3]{0,1:T(4,128)S(1)}, u32[]{:S(2)}, u32[]{:S(2)}) collective-permute-start(f32[32,3]{0,1:T(4,128)S(1)} %slice_select_fusion.6), channel_id=1, source_target_pairs={{0,1},{1,0},{2,3},{3,2},{4,5},{5,4},{6,7},{7,6},{8,9},{9,8},{10,11... | collective-permute-start | bytes 1160 | tf_op jit(solution)/shard_map/ppermute | solution.py:22
  270.6 1.9 collective-permute-start.7
  272.9 2.4 collective-permute-start.5
  275.6 0.6 collective-permute-done.5
  276.2 0.2 fusion.19
  276.4 0.6 copy.65
  (40 shorter events, 1.1 us)
Async XLA Ops:
  6.5 101.9 %copy-start = (bf16[1,1024,128]{2,1,0:T(8,128)(2,1)S(1)}, bf16[1,1024,128]{2,1,0:T(8,128)(2,1)}, u32[]{:S(2)}) copy-start(bf16[1,1024,128]{2,1,0:T(8,128)(2,1)} %param.8) | copy-start | bytes 786436
  6.5 98.4 %all-gather.2.cloned.1.call-start = ((), (), s32[]{:S(2)}) async-start(), calls=%async_computation.3 | async-start | bytes 1671168 | tf_op jit(solution)/shard_map/all_gather | solution.py:76
  6.5 10.0 %collective-permute-start = (bf16[32,384]{1,0:T(8,128)(2,1)}, bf16[32,384]{1,0:T(8,128)(2,1)S(1)}, u32[]{:S(2)}, u32[]{:S(2)}) collective-permute-start(bf16[32,384]{1,0:T(8,128)(2,1)} %param.7), channel_id=1, source_target_pairs={{0,1},{1,0},{2,3},{3,2},{4,5},{5,4},{6,7},{7,6},{8,9},{9,8},{10,11... | collective-permute-start | bytes 73736 | tf_op jit(solution)/shard_map/ppermute | solution.py:22
  17.3 4.8 %collective-permute-start.1 = (bf16[32,768]{1,0:T(8,128)(2,1)S(1)}, bf16[32,768]{1,0:T(8,128)(2,1)S(1)}, u32[]{:S(2)}, u32[]{:S(2)}) collective-permute-start(bf16[32,768]{1,0:T(8,128)(2,1)S(1)} %maximum_select_fusion.1), channel_id=1, source_target_pairs={{0,2},{2,0},{1,3},{3,1},{4,6},{6,4},{5,7},{7,5},{8,10},{10,8},{9,1... | collective-permute-start | bytes 147464 | tf_op jit(solution)/shard_map/ppermute | solution.py:22
  106.8 13.1 %copy-start.1 = (f32[512,12,8]{0,2,1:T(8,128)}, f32[512,12,8]{0,2,1:T(8,128)S(1)}, u32[]{:S(2)}) copy-start(f32[512,12,8]{0,2,1:T(8,128)S(1)} %get-tuple-element.21) | copy-start | bytes 589828
  120.7 11.7 %copy-start.3 = (bf16[1,1024,128]{2,1,0:T(8,128)(2,1)S(1)}, bf16[1,1024,128]{2,1,0:T(8,128)(2,1)}, u32[]{:S(2)}) copy-start(bf16[1,1024,128]{2,1,0:T(8,128)(2,1)} %param.9) | copy-start | bytes 786436
  132.4 32.0 %copy-start.2 = (bf16[1,8,128]{2,1,0:T(8,128)(2,1)S(1)}, bf16[1,8,128]{2,1,0:T(8,128)(2,1)}, u32[]{:S(2)}) copy-start(bf16[1,8,128]{2,1,0:T(8,128)(2,1)} %param.11) | copy-start | bytes 6148
  147.8 13.1 %all-to-all-start.2 = ((f32[16,1,384]{2,1,0:T(1,128)}), f32[16,1,384]{2,1,0:T(1,128)}, u32[]{:S(2)}, u32[]{:S(2)}) async-start(f32[16,1,384]{2,1,0:T(1,128)} %reshape.87), calls=%async_computation.2 | async-start | bytes 49152 | tf_op jit(solution)/shard_map/all_to_all | solution.py:87
  160.8 15.4 %all-to-all-start.1 = ((f32[16,1,384]{2,1,0:T(1,128)}), f32[16,1,384]{2,1,0:T(1,128)S(1)}, u32[]{:S(2)}, u32[]{:S(2)}) async-start(f32[16,1,384]{2,1,0:T(1,128)} %reshape.85), calls=%async_computation.1 | async-start | bytes 49152 | tf_op jit(solution)/shard_map/all_to_all | solution.py:86
  176.3 80.2 %all-to-all-start = ((f32[16,32,1536]{2,1,0:T(8,128)}), f32[16,32,1536]{2,1,0:T(8,128)}, u32[]{:S(2)}, u32[]{:S(2)}) async-start(f32[16,32,1536]{2,1,0:T(8,128)} %all_to_all.32), calls=%async_computation | async-start | bytes 6291456 | tf_op jit(solution)/shard_map/all_to_all | solution.py:85
  188.3 11.3 %collective-permute-start.2 = (f32[32,6]{0,1:T(8,128)S(1)}, f32[32,6]{0,1:T(8,128)S(1)}, u32[]{:S(2)}, u32[]{:S(2)}) collective-permute-start(f32[32,6]{0,1:T(8,128)S(1)} %slice_select_fusion.3), channel_id=1, source_target_pairs={{0,2},{2,0},{1,3},{3,1},{4,6},{6,4},{5,7},{7,5},{8,10},{10,8},{9,1... | collective-permute-start | bytes 2312 | tf_op jit(solution)/shard_map/ppermute | solution.py:22
  191.1 8.4 %collective-permute-start.6 = (f32[32,6]{0,1:T(8,128)S(1)}, f32[32,6]{0,1:T(8,128)S(1)}, u32[]{:S(2)}, u32[]{:S(2)}) collective-permute-start(f32[32,6]{0,1:T(8,128)S(1)} %slice_select_fusion.2), channel_id=1, source_target_pairs={{0,2},{2,0},{1,3},{3,1},{4,6},{6,4},{5,7},{7,5},{8,10},{10,8},{9,1... | collective-permute-start | bytes 2312 | tf_op jit(solution)/shard_map/ppermute | solution.py:22
  262.0 10.8 %collective-permute-start.3 = (f32[32,6,128]{2,1,0:T(8,128)S(1)}, f32[32,6,128]{2,1,0:T(8,128)S(1)}, u32[]{:S(2)}, u32[]{:S(2)}) collective-permute-start(f32[32,6,128]{2,1,0:T(8,128)S(1)} %slice_select_fusion), channel_id=1, source_target_pairs={{0,2},{2,0},{1,3},{3,1},{4,6},{6,4},{5,7},{7,5},{8,10},{10,8},{9,1... | collective-permute-start | bytes 294920 | tf_op jit(solution)/shard_map/ppermute | solution.py:22
  264.5 10.8 %collective-permute-start.4 = (f32[32,3]{0,1:T(4,128)S(1)}, f32[32,3]{0,1:T(4,128)S(1)}, u32[]{:S(2)}, u32[]{:S(2)}) collective-permute-start(f32[32,3]{0,1:T(4,128)S(1)} %slice_select_fusion.6), channel_id=1, source_target_pairs={{0,1},{1,0},{2,3},{3,2},{4,5},{5,4},{6,7},{7,6},{8,9},{9,8},{10,11... | collective-permute-start | bytes 1160 | tf_op jit(solution)/shard_map/ppermute | solution.py:22
  270.6 4.7 %collective-permute-start.7 = (f32[32,3]{0,1:T(4,128)S(1)}, f32[32,3]{0,1:T(4,128)S(1)}, u32[]{:S(2)}, u32[]{:S(2)}) collective-permute-start(f32[32,3]{0,1:T(4,128)S(1)} %slice_select_fusion.5), channel_id=1, source_target_pairs={{0,1},{1,0},{2,3},{3,2},{4,5},{5,4},{6,7},{7,6},{8,9},{9,8},{10,11... | collective-permute-start | bytes 1160 | tf_op jit(solution)/shard_map/ppermute | solution.py:22
  272.9 3.3 %collective-permute-start.5 = (f32[32,3,128]{2,1,0:T(4,128)S(1)}, f32[32,3,128]{2,1,0:T(4,128)S(1)}, u32[]{:S(2)}, u32[]{:S(2)}) collective-permute-start(f32[32,3,128]{2,1,0:T(4,128)S(1)} %slice_select_fusion.1), channel_id=1, source_target_pairs={{0,1},{1,0},{2,3},{3,2},{4,5},{5,4},{6,7},{7,6},{8,9},{9,8},{10,11... | collective-permute-start | bytes 147464 | tf_op jit(solution)/shard_map/ppermute | solution.py:22
Sparse Core Ops, SparseCore 0:
  23.0 81.9 all-gather.1
where the time goes:
time: 285 us; the launch traced here: 284 us
  waiting for transfers between devices  146 us (51%)
  starting transfers between devices  45.9 us (16%)
  matrix products  27.6 us (10%)
  local copies, waits for them, and re-layouts  26.8 us (9%)
  other arithmetic  22.8 us (8%)
  between operations  14.4 us (5%)
    all_gather x1, waiting for transfers between devices, body(): piece = lax.all_gather(group_q, 'ctx', axis=0, tiled=True)  79.9 us
    all_to_all x1, waiting for transfers between devices, body(): lax.all_to_all(flat, 'ctx', split_axis=0, concat_axis=1, tiled=True)  56.8 us
    ppermute x8, starting transfers between devices, swapped(): return lax.ppermute(block, axis, route)  29.3 us
    dot_general x2, matrix products, attend(): jnp.einsum('tgk,kd->tgd', weights.astype(jnp.bfloat16), values, preferred...  14.1 us
    dot_general x2, matrix products, attend(): jnp.einsum('tgd,kd->tgk', block_q, keys, preferred_element_type=jnp.float32)  13.5 us
    reduce_sum x2, other arithmetic, attend(): total = jnp.sum(weights, axis=2)  11.8 us
    all_to_all x1, starting transfers between devices, body(): lax.all_to_all(flat, 'ctx', split_axis=0, concat_axis=1, tiled=True)  9.03 us
    all_to_all x1, waiting for transfers between devices, body(): lax.all_to_all(total, 'ctx', split_axis=0, concat_axis=1, tiled=True)  5.77 us
  transfers between devices with their start and end apart: 12, of which 6 were waited for; matrix products, arithmetic and copies ran while one was open for 8% of the time, Pallas kernels for 0%

commit v1 on v0

v1 whole, which is shorter than its diff:
```python
import functools
import math

import jax
import jax.numpy as jnp
from jax import lax
from jax.experimental import pallas as pl
from jax.experimental.pallas import tpu as pltpu
from jax.sharding import PartitionSpec as P

Q_HEADS = 96
KV_HEADS = 8
NEGATIVE = -1e30
STEP = 256
TILE = 4
STAT_ROWS = 16

VMEM = pl.BlockSpec(memory_space=pltpu.VMEM)
SMEM = pl.BlockSpec(memory_space=pltpu.SMEM)


def prepare_kernel(fill_ref, k_ref, v_ref, tk_ref, tv_ref, kv_ref):
    slots, width = k_ref.shape
    turn = tk_ref.shape[0]
    fill = fill_ref[0]
    ok = lax.broadcasted_iota(jnp.int32, (slots, width), 0) < fill
    first = jnp.broadcast_to(k_ref[0:1, :].astype(jnp.float32), (slots, width))
    kv_ref[0:slots, :] = jnp.where(ok, k_ref[...].astype(jnp.float32), first).astype(jnp.bfloat16)
    kv_ref[slots : 2 * slots, :] = jnp.where(ok, v_ref[...].astype(jnp.float32), 0.0).astype(jnp.bfloat16)
    kv_ref[2 * slots : 2 * slots + 2 * turn, :] = jnp.concatenate([tk_ref[...], tv_ref[...]], axis=0)


def bias_kernel(index_ref, pos_smem, pos_ref, bias_ref):
    blocks, width = pos_ref.shape
    ctx, sub = index_ref[0], index_ref[1]
    lane = lax.broadcasted_iota(jnp.int32, (1, width), 1)
    keys = jnp.full((1, width), 1 << 20, jnp.int32)
    for n, flip in enumerate((0, 2, 1, 3)):
        base = (sub ^ flip) * width + ctx * 8
        for i in range(8):
            keys = jnp.where(lane == n * 8 + i, pos_smem[base + i], keys)
    keys = keys.astype(jnp.float32)
    pos = pos_ref[...].astype(jnp.float32)
    for b in range(blocks):
        tokens = jnp.broadcast_to(pos[b : b + 1, :], (width, width)).T
        bias_ref[b * width : (b + 1) * width, :] = jnp.where(keys <= tokens, 0.0, NEGATIVE)


def attend_kernel(fill_ref, q_ref, a_ref, b_ref, c_ref, d_ref, bias_ref, out_ref, *, slots, turn):
    sources = (a_ref, b_ref, c_ref, d_ref)
    blocks, tokens, columns = q_ref.shape
    width = a_ref.shape[1]
    heads = columns // width
    rows = heads * tokens
    factor = math.log2(math.e) / math.sqrt(width)
    fill = fill_ref[0]
    steps = (fill + (STEP - 1)) // STEP
    contract = (((1,), (1,)), ((), ()))
    plain = (((1,), (0,)), ((), ()))

    def scored(q, keys):
        return lax.dot_general(q, keys, contract, preferred_element_type=jnp.float32)

    def flags(start):
        at = lax.broadcasted_iota(jnp.int32, (STEP, width), 0) + start
        return jnp.where(at < fill, 1.0, 0.0).astype(jnp.bfloat16)

    def weighted(scores, peak, values):
        weights = jnp.exp2(scores - peak).astype(jnp.bfloat16)
        return lax.dot_general(weights, values, plain, preferred_element_type=jnp.float32)

    turn_k = jnp.concatenate([s[2 * slots : 2 * slots + 2 * turn, :][:turn] for s in sources], axis=0)
    turn_v = jnp.concatenate([s[2 * slots : 2 * slots + 2 * turn, :][turn:] for s in sources], axis=0)
    count = turn * len(sources)
    turn_va = jnp.concatenate([turn_v, jnp.ones((count, width), jnp.bfloat16)], axis=1)

    def tile(at, _):
        q = jnp.concatenate(
            [q_ref[at * TILE + n, :, h * width : (h + 1) * width] for n in range(TILE) for h in range(heads)], axis=0
        )
        bias = jnp.concatenate(
            [
                bias_ref[pl.ds(pl.multiple_of((at * TILE + n) * tokens, tokens), tokens), 0:count]
                for n in range(TILE)
                for h in range(heads)
            ],
            axis=0,
        )

        def step(start):
            return [scored(q, s[pl.ds(start, STEP), :]) * factor for s in sources]

        def peak_of(scores):
            best = functools.reduce(jnp.maximum, scores)
            return jnp.max(best, axis=1, keepdims=True)

        def mixed(scores, peak, start):
            flag = flags(start)
            return sum(
                weighted(
                    x,
                    peak,
                    jnp.concatenate([s[pl.ds(pl.multiple_of(slots + start, STEP), STEP), :], flag], axis=1),
                )
                for x, s in zip(scores, sources)
            )

        scores = step(0)
        fresh = scored(q, turn_k) * factor + bias
        peak = jnp.maximum(peak_of(scores), jnp.max(fresh, axis=1, keepdims=True))
        total = mixed(scores, peak, 0) + weighted(fresh, peak, turn_va)

        def more(j, state):
            total, peak = state
            start = pl.multiple_of(j * STEP, STEP)
            scores = step(start)
            best = jnp.maximum(peak, peak_of(scores))
            return total * jnp.exp2(peak - best) + mixed(scores, best, start), best

        total, peak = lax.fori_loop(1, steps, more, (total, peak))
        norm = total[:, width:]
        result = (total[:, :width] / norm).astype(jnp.bfloat16)
        lse = peak + jnp.log2(norm)
        row = lax.broadcasted_iota(jnp.int32, (rows, width), 0)
        lane = lax.broadcasted_iota(jnp.int32, (rows, width), 1)
        stat_row = lax.broadcasted_iota(jnp.int32, (STAT_ROWS, width), 0)
        for n in range(TILE):
            out_ref[at * TILE + n, 0:rows, :] = result[n * rows : (n + 1) * rows]
            flat = jnp.sum(jnp.where(row == lane, lse[n * rows : (n + 1) * rows], 0.0), axis=0, keepdims=True)
            high = flat.astype(jnp.bfloat16).astype(jnp.float32)
            middle = (flat - high).astype(jnp.bfloat16).astype(jnp.float32)
            low = flat - high - middle
            stat = jnp.where(
                stat_row == 0, high, jnp.where(stat_row == 1, middle, jnp.where(stat_row == 2, low, 0.0))
            )
            out_ref[at * TILE + n, rows : rows + STAT_ROWS, :] = stat.astype(jnp.bfloat16)
        return 0

    lax.fori_loop(0, blocks // TILE, tile, 0)


def combine_kernel(part_ref, out_ref):
    blocks, _, width = part_ref.shape
    tokens, columns = out_ref.shape
    heads = columns // width
    rows = heads * tokens
    pieces = [part_ref[c, rows : rows + STAT_ROWS, :].astype(jnp.float32) for c in range(blocks)]
    lse = jnp.concatenate([p[0:1] + p[1:2] + p[2:3] for p in pieces], axis=0)
    share = jnp.exp2(lse - jnp.max(lse, axis=0, keepdims=True))
    share = share / jnp.sum(share, axis=0, keepdims=True)
    share = jnp.concatenate([share, jnp.zeros((width - blocks, width), jnp.float32)], axis=0).T
    total = jnp.zeros((rows, width), jnp.float32)
    for c in range(blocks):
        total = total + part_ref[c, 0:rows, :].astype(jnp.float32) * share[0:rows, c : c + 1]
    total = total.astype(jnp.bfloat16)
    for h in range(heads):
        out_ref[:, h * width : (h + 1) * width] = total[h * tokens : (h + 1) * tokens]


def prepare(fill, keys, values, turn_k, turn_v):
    slots, width = keys.shape
    return pl.pallas_call(
        prepare_kernel,
        out_shape=jax.ShapeDtypeStruct((2 * slots + 2 * turn_k.shape[0], width), jnp.bfloat16),
        in_specs=[SMEM] + [VMEM] * 4,
        out_specs=VMEM,
        name="prepare",
    )(fill, keys, values, turn_k, turn_v)


def bias_of(index, positions, width):
    return pl.pallas_call(
        bias_kernel,
        out_shape=jax.ShapeDtypeStruct((positions.shape[0], width), jnp.float32),
        in_specs=[SMEM, SMEM, VMEM],
        out_specs=VMEM,
        name="bias",
    )(index, positions, positions.reshape(-1, width))


def attend(fill, q, sources, bias, slots, turn):
    blocks, tokens, columns = q.shape
    width = bias.shape[1]
    rows = tokens * columns // width
    work = blocks * rows * slots * len(sources)
    return pl.pallas_call(
        functools.partial(attend_kernel, slots=slots, turn=turn),
        out_shape=jax.ShapeDtypeStruct((blocks, rows + STAT_ROWS, width), jnp.bfloat16),
        in_specs=[SMEM] + [VMEM] * 6,
        out_specs=VMEM,
        compiler_params=pltpu.CompilerParams(vmem_limit_bytes=48 * 1024 * 1024),
        cost_estimate=pl.CostEstimate(flops=4 * work * width, bytes_accessed=4 << 20, transcendentals=work),
        name="attend",
    )(fill, q, *sources, bias)


def combine(parts, tokens, columns):
    return pl.pallas_call(
        combine_kernel,
        out_shape=jax.ShapeDtypeStruct((tokens, columns), jnp.bfloat16),
        in_specs=[VMEM],
        out_specs=VMEM,
        name="combine",
    )(parts)


def body(queries, cache_keys, cache_values, turn_keys, turn_values, cache_fill, turn_positions):
    tokens, columns = queries.shape
    width = cache_keys.shape[2]
    slots = cache_keys.shape[1]
    turn = turn_keys.shape[1]
    n_ctx, n_head = lax.axis_size("ctx"), lax.axis_size("head")
    sub = lax.axis_index("head") % (n_head // KV_HEADS)
    index = jnp.stack([lax.axis_index("ctx"), sub]).astype(jnp.int32)
    other = [(i, i ^ 1) for i in range(n_head)]
    across = [(i, i ^ 2) for i in range(n_head)]

    copies = jnp.broadcast_to(queries[None], (n_ctx, tokens, columns))
    q = lax.all_to_all(copies, "ctx", split_axis=0, concat_axis=0, tiled=True)
    own = prepare(cache_fill, cache_keys[0], cache_values[0], turn_keys[0], turn_values[0])
    far = lax.ppermute(own, "head", across)
    near = lax.ppermute(own, "head", other)
    diagonal = lax.ppermute(far, "head", other)
    bias = bias_of(index, turn_positions, width)
    parts = attend(cache_fill, q, (own, far, near, diagonal), bias, slots, turn)
    parts = lax.all_to_all(parts, "ctx", split_axis=0, concat_axis=0, tiled=True)
    return combine(parts, tokens, columns)


def solution(mesh):
    in_specs = (
        P("ctx", "head"),
        P("head", "ctx", None),
        P("head", "ctx", None),
        P("head", "ctx", None),
        P("head", "ctx", None),
        P("ctx"),
        P(),
    )
    return jax.shard_map(body, mesh=mesh, in_specs=in_specs, out_specs=P("ctx", "head"), check_vma=False)
```

time: 285 us -> 74.9 us (0.26)
  the two profiles are of different devices: /device:TPU:1 before, /device:TPU:448 now
where the time goes in v1:
time: 74.9 us; the launch traced here: 74.5 us
  Pallas kernels  25.5 us (34%)
  blocking collectives  19.4 us (26%)
  starting transfers between devices  16.7 us (22%)
  waiting for transfers between devices  9.74 us (13%)
  local copies, waits for them, and re-layouts  1.74 us (2%)
    pallas_call x1, Pallas kernels, attend(): pl.pallas_call(functools.partial(attend_kernel, slots=slots, turn=turn),...  19.8 us
    all_to_all x1, blocking collectives, body(): lax.all_to_all(parts, 'ctx', split_axis=0, concat_axis=0, tiled=True)  19.4 us
    all_to_all x1, starting transfers between devices, body(): q = lax.all_to_all(copies, 'ctx', split_axis=0, concat_axis=0, tiled=True)  9.37 us
    all_to_all x1, waiting for transfers between devices, body(): q = lax.all_to_all(copies, 'ctx', split_axis=0, concat_axis=0, tiled=True)  9.13 us
    ppermute x1, starting transfers between devices, body(): far = lax.ppermute(own, 'head', across)  3.52 us
    pallas_call x1, Pallas kernels, combine(): pl.pallas_call(combine_kernel, out_shape=jax.ShapeDtypeStruct((tokens, co...  2.08 us
    pallas_call x1, Pallas kernels, prepare(): pl.pallas_call(prepare_kernel, out_shape=jax.ShapeDtypeStruct((2 * slots...  2.01 us
    ppermute x1, starting transfers between devices, body(): near = lax.ppermute(own, 'head', other)  1.92 us
  transfers between devices with their start and end apart: 4, of which 2 were waited for; matrix products, arithmetic and copies ran while one was open for 2% of the time, Pallas kernels for 2%

profile of v1, /device:TPU:448, one launch (start us, length us, event | category | flops | bytes accessed | tf_op | source)
XLA Modules:
  0.0 74.5 jit_solution(3906072011104726627)
XLA Ops:
  0.7 0.0 copy-start.2
  0.7 2.0 %prepare.1.a_ref = bf16[2064,128]{1,0:T(8,128)(2,1)} custom-call(s32[1]{0:T(128)S(6)} %copy.8.fill_ref, bf16[1024,128]{1,0:T(8,128)(2,1)} %bitcast.7, bf16[1024,128]{1,0:T(8,128)(2,1)} %bitcast.8, bf16[8,128]{1,0:T(8,128)(2,1)} %bitcast.10, bf16[8,128]{1,0:T(8,128)(2,1)} %bitcast.11), custom_call_target="tpu_custom_call" | custom-call | tf_op jit(solution)/shard_map/prepare/pallas_call | solution.py:162
  2.7 0.0 copy-start
  2.7 3.5 %collective-permute-start = (bf16[2064,128]{1,0:T(8,128)(2,1)}, bf16[2064,128]{1,0:T(8,128)(2,1)S(1)}, u32[]{:S(2)}, u32[]{:S(2)}) collective-permute-start(bf16[2064,128]{1,0:T(8,128)(2,1)} %prepare.1.a_ref), channel_id=1, source_target_pairs={{0,2},{1,3},{2,0},{3,1},{4,6},{5,7},{6,4},{7,5},{8,10},{9,11},{10,... | collective-permute-start | bytes 1585160 | tf_op jit(solution)/shard_map/ppermute | solution.py:221
  6.2 0.0 copy-done.2
  6.2 0.8 %broadcast_in_dim.2 = bf16[16,32,384]{2,1,0:T(8,128)(2,1)} broadcast(bf16[32,384]{1,0:T(8,128)(2,1)S(1)} %copy-done.2), dimensions={1,2} | broadcast | bytes 417792 | tf_op jit(solution)/shard_map/broadcast_in_dim | solution.py:218
  7.0 9.4 %all-to-all-start = ((bf16[16,32,384]{2,1,0:T(8,128)(2,1)}), bf16[16,32,384]{2,1,0:T(8,128)(2,1)S(1)}, u32[]{:S(2)}, u32[]{:S(2)}) async-start(bf16[16,32,384]{2,1,0:T(8,128)(2,1)} %broadcast_in_dim.2), calls=%async_computation | async-start | bytes 786432 | tf_op jit(solution)/shard_map/all_to_all | solution.py:219
  16.4 0.0 copy-done
  16.4 1.9 %collective-permute-start.1 = (bf16[2064,128]{1,0:T(8,128)(2,1)S(1)}, bf16[2064,128]{1,0:T(8,128)(2,1)S(1)}, u32[]{:S(2)}, u32[]{:S(2)}) collective-permute-start(bf16[2064,128]{1,0:T(8,128)(2,1)S(1)} %copy-done), channel_id=1, source_target_pairs={{0,1},{1,0},{2,3},{3,2},{4,5},{5,4},{6,7},{7,6},{8,9},{9,8},{10,11... | collective-permute-start | bytes 1585160 | tf_op jit(solution)/shard_map/ppermute | solution.py:222
  18.3 0.6 collective-permute-done.b_ref
  18.9 1.9 %collective-permute-start.2 = (bf16[2064,128]{1,0:T(8,128)(2,1)S(1)}, bf16[2064,128]{1,0:T(8,128)(2,1)S(1)}, u32[]{:S(2)}, u32[]{:S(2)}) collective-permute-start(bf16[2064,128]{1,0:T(8,128)(2,1)S(1)} %collective-permute-done.b_ref), channel_id=1, source_target_pairs={{0,1},{1,0},{2,3},{3,2},{4,5},{5,4},{6,7},{7,6},{8,9},{9,8},{10,11... | collective-permute-start | bytes 1585160 | tf_op jit(solution)/shard_map/ppermute | solution.py:223
  20.8 0.7 pad_add_fusion.index_ref
  21.5 1.6 %bias.1.bias_ref = f32[512,128]{1,0:T(8,128)} custom-call(s32[2]{0:T(128)} %pad_add_fusion.index_ref, s32[512]{0:T(512)} %pos_smem.1, s32[4,128]{1,0:T(4,128)} %bitcast.9), custom_call_target="tpu_custom_call" | custom-call | tf_op jit(solution)/shard_map/bias/pallas_call | solution.py:172
  23.1 0.0 collective-permute-done.1.c_ref
  23.1 9.1 %all-to-all-done.q_ref = bf16[16,32,384]{2,1,0:T(8,128)(2,1)S(1)} async-done(((bf16[16,32,384]{2,1,0:T(8,128)(2,1)}), bf16[16,32,384]{2,1,0:T(8,128)(2,1)S(1)}, u32[]{:S(2)}, u32[]{:S(2)}) %all-to-all-start) | async-done | bytes 393248 | tf_op jit(solution)/shard_map/all_to_all | solution.py:219
  32.2 0.0 collective-permute-done.2.d_ref
  32.2 0.0 copy-start.1
  32.2 0.9 %copy-done.1 = f32[512,128]{1,0:T(8,128)S(1)} copy-done((f32[512,128]{1,0:T(8,128)S(1)}, f32[512,128]{1,0:T(8,128)}, u32[]{:S(2)}) %copy-start.1) | copy-done | bytes 262168
  33.2 19.8 %attend.1 = bf16[16,112,128]{2,1,0:T(8,128)(2,1)S(1)} custom-call(s32[1]{0:T(128)S(6)} %copy.8.fill_ref, bf16[16,32,384]{2,1,0:T(8,128)(2,1)S(1)} %all-to-all-done.q_ref, bf16[2064,128]{1,0:T(8,128)(2,1)S(1)} %copy-done, bf16[2064,128]{1,0:T(8,128)(2,1)S(1)} %collective-permute-done.b_ref, bf16[2064,128]{1,0:T(8,128)(2,1)S(1)} %collective-permute-done.1.c_ref, ...), custom_call_target="tpu_custom_call" | custom-call | flops 3221225472 | bytes 4194304 | tf_op jit(solution)/shard_map/attend/pallas_call | solution.py:186
  53.0 19.4 %all_to_all.10.part_ref = bf16[16,112,128]{2,1,0:T(8,128)(2,1)} all-to-all(bf16[16,112,128]{2,1,0:T(8,128)(2,1)S(1)} %attend.1), channel_id=1, replica_groups=mesh['ctx'=16,'head'=32] {'ctx'}, dimensions={0} | all-to-all | bytes 917504 | tf_op jit(solution)/shard_map/all_to_all | solution.py:226
  72.4 2.1 %combine.1 = bf16[32,384]{1,0:T(8,128)(2,1)} custom-call(bf16[16,112,128]{2,1,0:T(8,128)(2,1)} %all_to_all.10.part_ref), custom_call_target="tpu_custom_call" | custom-call | tf_op jit(solution)/shard_map/combine/pallas_call | solution.py:198
Async XLA Ops:
  0.7 5.6 %copy-start.2 = (bf16[32,384]{1,0:T(8,128)(2,1)S(1)}, bf16[32,384]{1,0:T(8,128)(2,1)}, u32[]{:S(2)}) copy-start(bf16[32,384]{1,0:T(8,128)(2,1)} %param.7) | copy-start | bytes 73732
  2.7 13.7 %copy-start = (bf16[2064,128]{1,0:T(8,128)(2,1)S(1)}, bf16[2064,128]{1,0:T(8,128)(2,1)}, u32[]{:S(2)}) copy-start(bf16[2064,128]{1,0:T(8,128)(2,1)} %prepare.1.a_ref) | copy-start | bytes 1585156
  2.7 16.2 %collective-permute-start = (bf16[2064,128]{1,0:T(8,128)(2,1)}, bf16[2064,128]{1,0:T(8,128)(2,1)S(1)}, u32[]{:S(2)}, u32[]{:S(2)}) collective-permute-start(bf16[2064,128]{1,0:T(8,128)(2,1)} %prepare.1.a_ref), channel_id=1, source_target_pairs={{0,2},{1,3},{2,0},{3,1},{4,6},{5,7},{6,4},{7,5},{8,10},{9,11},{10,... | collective-permute-start | bytes 1585160 | tf_op jit(solution)/shard_map/ppermute | solution.py:221
  7.0 25.2 %all-to-all-start = ((bf16[16,32,384]{2,1,0:T(8,128)(2,1)}), bf16[16,32,384]{2,1,0:T(8,128)(2,1)S(1)}, u32[]{:S(2)}, u32[]{:S(2)}) async-start(bf16[16,32,384]{2,1,0:T(8,128)(2,1)} %broadcast_in_dim.2), calls=%async_computation | async-start | bytes 786432 | tf_op jit(solution)/shard_map/all_to_all | solution.py:219
  16.4 6.7 %collective-permute-start.1 = (bf16[2064,128]{1,0:T(8,128)(2,1)S(1)}, bf16[2064,128]{1,0:T(8,128)(2,1)S(1)}, u32[]{:S(2)}, u32[]{:S(2)}) collective-permute-start(bf16[2064,128]{1,0:T(8,128)(2,1)S(1)} %copy-done), channel_id=1, source_target_pairs={{0,1},{1,0},{2,3},{3,2},{4,5},{5,4},{6,7},{7,6},{8,9},{9,8},{10,11... | collective-permute-start | bytes 1585160 | tf_op jit(solution)/shard_map/ppermute | solution.py:222
  18.9 13.3 %collective-permute-start.2 = (bf16[2064,128]{1,0:T(8,128)(2,1)S(1)}, bf16[2064,128]{1,0:T(8,128)(2,1)S(1)}, u32[]{:S(2)}, u32[]{:S(2)}) collective-permute-start(bf16[2064,128]{1,0:T(8,128)(2,1)S(1)} %collective-permute-done.b_ref), channel_id=1, source_target_pairs={{0,1},{1,0},{2,3},{3,2},{4,5},{5,4},{6,7},{7,6},{8,9},{9,8},{10,11... | collective-permute-start | bytes 1585160 | tf_op jit(solution)/shard_map/ppermute | solution.py:223
  32.2 1.0 %copy-start.1 = (f32[512,128]{1,0:T(8,128)S(1)}, f32[512,128]{1,0:T(8,128)}, u32[]{:S(2)}) copy-start(f32[512,128]{1,0:T(8,128)} %bias.1.bias_ref) | copy-start | bytes 786436

commit v2 on v1

--- a/solution.py
+++ b/solution.py
@@ -11,8 +11,10 @@
 Q_HEADS = 96
 KV_HEADS = 8
 NEGATIVE = -1e30
-STEP = 256
-TILE = 4
+STEP = 512
+TILE = 2
+AHEAD = 3
+KERNEL_VMEM = 24 * 1024 * 1024
 STAT_ROWS = 16
 
 VMEM = pl.BlockSpec(memory_space=pltpu.VMEM)
@@ -23,10 +25,13 @@
     slots, width = k_ref.shape
     turn = tk_ref.shape[0]
     fill = fill_ref[0]
-    ok = lax.broadcasted_iota(jnp.int32, (slots, width), 0) < fill
-    first = jnp.broadcast_to(k_ref[0:1, :].astype(jnp.float32), (slots, width))
-    kv_ref[0:slots, :] = jnp.where(ok, k_ref[...].astype(jnp.float32), first).astype(jnp.bfloat16)
-    kv_ref[slots : 2 * slots, :] = jnp.where(ok, v_ref[...].astype(jnp.float32), 0.0).astype(jnp.bfloat16)
+    first = jnp.broadcast_to(k_ref[0:1, :].astype(jnp.float32), (width, width))
+    for at in range(0, slots, width):
+        ok = lax.broadcasted_iota(jnp.int32, (width, width), 0) + at < fill
+        keys = jnp.where(ok, k_ref[at : at + width, :].astype(jnp.float32), first)
+        kv_ref[at : at + width, :] = keys.T.astype(jnp.bfloat16)
+        values = jnp.where(ok, v_ref[at : at + width, :].astype(jnp.float32), 0.0)
+        kv_ref[slots + at : slots + at + width, :] = values.astype(jnp.bfloat16)
     kv_ref[2 * slots : 2 * slots + 2 * turn, :] = jnp.concatenate([tk_ref[...], tv_ref[...]], axis=0)
 
 
@@ -46,97 +51,112 @@
         bias_ref[b * width : (b + 1) * width, :] = jnp.where(keys <= tokens, 0.0, NEGATIVE)
 
 
-def attend_kernel(fill_ref, q_ref, a_ref, b_ref, c_ref, d_ref, bias_ref, out_ref, *, slots, turn):
+def attend_kernel(
+    fill_ref, q_ref, a_ref, b_ref, c_ref, d_ref, bias_ref, out_ref, total_ref, peak_ref, *, slots, turn
+):
     sources = (a_ref, b_ref, c_ref, d_ref)
     blocks, tokens, columns = q_ref.shape
     width = a_ref.shape[1]
     heads = columns // width
     rows = heads * tokens
+    size = TILE * rows
+    tiles = blocks // TILE
+    count = turn * len(sources)
     factor = math.log2(math.e) / math.sqrt(width)
     fill = fill_ref[0]
-    steps = (fill + (STEP - 1)) // STEP
+    plain = (((1,), (0,)), ((), ()))
     contract = (((1,), (1,)), ((), ()))
-    plain = (((1,), (0,)), ((), ()))
-
-    def scored(q, keys):
-        return lax.dot_general(q, keys, contract, preferred_element_type=jnp.float32)
-
-    def flags(start):
-        at = lax.broadcasted_iota(jnp.int32, (STEP, width), 0) + start
-        return jnp.where(at < fill, 1.0, 0.0).astype(jnp.bfloat16)
-
-    def weighted(scores, peak, values):
-        weights = jnp.exp2(scores - peak).astype(jnp.bfloat16)
-        return lax.dot_general(weights, values, plain, preferred_element_type=jnp.float32)
-
-    turn_k = jnp.concatenate([s[2 * slots : 2 * slots + 2 * turn, :][:turn] for s in sources], axis=0)
-    turn_v = jnp.concatenate([s[2 * slots : 2 * slots + 2 * turn, :][turn:] for s in sources], axis=0)
-    count = turn * len(sources)
-    turn_va = jnp.concatenate([turn_v, jnp.ones((count, width), jnp.bfloat16)], axis=1)
-
-    def tile(at, _):
-        q = jnp.concatenate(
-            [q_ref[at * TILE + n, :, h * width : (h + 1) * width] for n in range(TILE) for h in range(heads)], axis=0
-        )
-        bias = jnp.concatenate(
-            [
-                bias_ref[pl.ds(pl.multiple_of((at * TILE + n) * tokens, tokens), tokens), 0:count]
-                for n in range(TILE)
-                for h in range(heads)
-            ],
-            axis=0,
-        )
-
-        def step(start):
-            return [scored(q, s[pl.ds(start, STEP), :]) * factor for s in sources]
-
-        def peak_of(scores):
-            best = functools.reduce(jnp.maximum, scores)
-            return jnp.max(best, axis=1, keepdims=True)
-
-        def mixed(scores, peak, start):
-            flag = flags(start)
-            return sum(
-                weighted(
-                    x,
-                    peak,
-                    jnp.concatenate([s[pl.ds(pl.multiple_of(slots + start, STEP), STEP), :], flag], axis=1),
-                )
-                for x, s in zip(scores, sources)
-            )
-
-        scores = step(0)
-        fresh = scored(q, turn_k) * factor + bias
-        peak = jnp.maximum(peak_of(scores), jnp.max(fresh, axis=1, keepdims=True))
-        total = mixed(scores, peak, 0) + weighted(fresh, peak, turn_va)
-
-        def more(j, state):
-            total, peak = state
-            start = pl.multiple_of(j * STEP, STEP)
-            scores = step(start)
-            best = jnp.maximum(peak, peak_of(scores))
-            return total * jnp.exp2(peak - best) + mixed(scores, best, start), best
-
-        total, peak = lax.fori_loop(1, steps, more, (total, peak))
-        norm = total[:, width:]
-        result = (total[:, :width] / norm).astype(jnp.bfloat16)
-        lse = peak + jnp.log2(norm)
-        row = lax.broadcasted_iota(jnp.int32, (rows, width), 0)
-        lane = lax.broadcasted_iota(jnp.int32, (rows, width), 1)
-        stat_row = lax.broadcasted_iota(jnp.int32, (STAT_ROWS, width), 0)
+
+    def dot(first, second, dims=plain):
+        return lax.dot_general(first, second, dims, preferred_element_type=jnp.float32)
+
+    def weights(scores, peak):
+        return jnp.exp2(scores * factor - peak).astype(jnp.bfloat16)
+
+    def turned(index):
+        pairs = [s[2 * slots : 2 * slots + 2 * turn, :] for s in sources]
+        return jnp.concatenate([p[index * turn : (index + 1) * turn] for p in pairs], axis=0)
+
+    turn_k = turned(0)
+    turn_v = jnp.concatenate([turned(1), jnp.ones((count, width), jnp.bfloat16)], axis=1)
+
+    row = lax.broadcasted_iota(jnp.int32, (rows, width), 0)
+    lane = lax.broadcasted_iota(jnp.int32, (rows, width), 1)
+    stat_row = lax.broadcasted_iota(jnp.int32, (STAT_ROWS, width), 0)
+
+    def finish(t, total, peak):
         for n in range(TILE):
-            out_ref[at * TILE + n, 0:rows, :] = result[n * rows : (n + 1) * rows]
-            flat = jnp.sum(jnp.where(row == lane, lse[n * rows : (n + 1) * rows], 0.0), axis=0, keepdims=True)
+            at = t * TILE + n
+            part = total[n * rows : (n + 1) * rows]
+            norm = part[:, width:]
+            out_ref[at, 0:rows, :] = (part[:, :width] / norm).astype(jnp.bfloat16)
+            lse = peak[n * rows : (n + 1) * rows] + jnp.log2(norm)
+            flat = jnp.sum(jnp.where(row == lane, lse, 0.0), axis=0, keepdims=True)
             high = flat.astype(jnp.bfloat16).astype(jnp.float32)
             middle = (flat - high).astype(jnp.bfloat16).astype(jnp.float32)
             low = flat - high - middle
             stat = jnp.where(
                 stat_row == 0, high, jnp.where(stat_row == 1, middle, jnp.where(stat_row == 2, low, 0.0))
             )
-            out_ref[at * TILE + n, rows : rows + STAT_ROWS, :] = stat.astype(jnp.bfloat16)
-        return 0
-
-    lax.fori_loop(0, blocks // TILE, tile, 0)
+            out_ref[at, rows : rows + STAT_ROWS, :] = stat.astype(jnp.bfloat16)
+
+    def step(start, first, last):
+        keys = jnp.concatenate([s[start + b : start + b + width, :] for s in sources for b in range(0, STEP, width)], axis=1)
+        slot = lax.broadcasted_iota(jnp.int32, (STEP, width), 0) + start
+        flag = jnp.where(slot < fill, 1.0, 0.0).astype(jnp.bfloat16)
+        values = jnp.concatenate(
+            [jnp.concatenate([s[slots + start : slots + start + STEP, :], flag], axis=1) for s in sources], axis=0
+        )
+
+        def score(t):
+            q = jnp.concatenate(
+                [q_ref[t * TILE + n, :, h * width : (h + 1) * width] for n in range(TILE) for h in range(heads)],
+                axis=0,
+            )
+            if not first:
+                return dot(q, keys), None
+            bias = jnp.concatenate(
+                [
+                    bias_ref[(t * TILE + n) * tokens : (t * TILE + n + 1) * tokens, 0:count]
+                    for n in range(TILE)
+                    for h in range(heads)
+                ],
+                axis=0,
+            )
+            return dot(q, keys), dot(q, turn_k, contract) + bias
+
+        def mix(t, scores, fresh):
+            at = slice(t * size, (t + 1) * size)
+            peak = jnp.max(scores, axis=1, keepdims=True)
+            if first:
+                peak = jnp.maximum(peak, jnp.max(fresh, axis=1, keepdims=True)) * factor
+                total = dot(weights(scores, peak), values) + dot(weights(fresh, peak), turn_v)
+            else:
+                before = peak_ref[at, 0:1]
+                peak = jnp.maximum(before, peak * factor)
+                total = total_ref[at, :] * jnp.exp2(before - peak) + dot(weights(scores, peak), values)
+            if last:
+                finish(t, total, peak)
+            else:
+                total_ref[at, :] = total
+                peak_ref[at, :] = jnp.broadcast_to(peak, (size, width))
+
+        ahead = []
+        for t in range(tiles):
+            ahead.append((t, *score(t)))
+            if len(ahead) > AHEAD:
+                mix(*ahead.pop(0))
+        for waiting in ahead:
+            mix(*waiting)
+
+    @pl.when(fill <= STEP)
+    def _():
+        step(0, True, True)
+
+    @pl.when(fill > STEP)
+    def _():
+        for start in range(0, slots, STEP):
+            step(start, start == 0, start + STEP == slots)
 
 
 def combine_kernel(part_ref, out_ref):
@@ -188,7 +208,11 @@
         out_shape=jax.ShapeDtypeStruct((blocks, rows + STAT_ROWS, width), jnp.bfloat16),
         in_specs=[SMEM] + [VMEM] * 6,
         out_specs=VMEM,
-        compiler_params=pltpu.CompilerParams(vmem_limit_bytes=48 * 1024 * 1024),
+        scratch_shapes=[
+            pltpu.VMEM((blocks * rows, 2 * width), jnp.float32),
+            pltpu.VMEM((blocks * rows, width), jnp.float32),
+        ],
+        compiler_params=pltpu.CompilerParams(vmem_limit_bytes=KERNEL_VMEM),
         cost_estimate=pl.CostEstimate(flops=4 * work * width, bytes_accessed=4 << 20, transcendentals=work),
         name="attend",
     )(fill, q, *sources, bias)
@@ -216,6 +240,7 @@
     across = [(i, i ^ 2) for i in range(n_head)]
 
     copies = jnp.broadcast_to(queries[None], (n_ctx, tokens, columns))
+    copies, cache_fill = lax.optimization_barrier((copies, cache_fill))
     q = lax.all_to_all(copies, "ctx", split_axis=0, concat_axis=0, tiled=True)
     own = prepare(cache_fill, cache_keys[0], cache_values[0], turn_keys[0], turn_values[0])
     far = lax.ppermute(own, "head", across)

time: 74.9 us -> 63 us (0.84)
  Pallas kernels: 25.5 us -> 13.9 us
    pallas_call x1, Pallas kernels: 19.8 us -> 8.23 us  [attend(): pl.pallas_call(functools.partial(attend_kernel, slots=slots, turn=turn),...]
where the time goes in v2:
time: 63 us; the launch traced here: 62.6 us
  blocking collectives  19.1 us (30%)
  starting transfers between devices  16.7 us (27%)
  Pallas kernels  13.9 us (22%)
  waiting for transfers between devices  9.74 us (15%)
  local copies, waits for them, and re-layouts  1.74 us (3%)
  between operations  0.73 us (1%)
  other arithmetic  0.65 us (1%)
    all_to_all x1, blocking collectives, body(): lax.all_to_all(parts, 'ctx', split_axis=0, concat_axis=0, tiled=True)  19.1 us
    all_to_all x1, starting transfers between devices, body(): q = lax.all_to_all(copies, 'ctx', split_axis=0, concat_axis=0, tiled=True)  9.37 us
    all_to_all x1, waiting for transfers between devices, body(): q = lax.all_to_all(copies, 'ctx', split_axis=0, concat_axis=0, tiled=True)  9.13 us
    pallas_call x1, Pallas kernels, attend(): pl.pallas_call(functools.partial(attend_kernel, slots=slots, turn=turn),...  8.23 us
    ppermute x1, starting transfers between devices, body(): far = lax.ppermute(own, 'head', across)  3.52 us
    pallas_call x1, Pallas kernels, combine(): pl.pallas_call(combine_kernel, out_shape=jax.ShapeDtypeStruct((tokens, co...  2.08 us
    pallas_call x1, Pallas kernels, prepare(): pl.pallas_call(prepare_kernel, out_shape=jax.ShapeDtypeStruct((2 * slots...  2.04 us
    ppermute x1, starting transfers between devices, body(): near = lax.ppermute(own, 'head', other)  1.92 us
  transfers between devices with their start and end apart: 4, of which 2 were waited for; matrix products, arithmetic and copies ran while one was open for 2% of the time, Pallas kernels for 2%

profile of v2, /device:TPU:448, one launch (start us, length us, event | category | flops | bytes accessed | tf_op | source)
XLA Modules:
  0.0 62.6 jit_solution(6961478532191496705)
XLA Ops:
  0.7 0.0 copy-start.2
  0.7 2.0 %prepare.1.a_ref = bf16[2064,128]{1,0:T(8,128)(2,1)} custom-call(s32[1]{0:T(128)S(6)} %copy.8.fill_ref, bf16[1024,128]{1,0:T(8,128)(2,1)} %bitcast.7, bf16[1024,128]{1,0:T(8,128)(2,1)} %bitcast.8, bf16[8,128]{1,0:T(8,128)(2,1)} %bitcast.10, bf16[8,128]{1,0:T(8,128)(2,1)} %bitcast.11), custom_call_target="tpu_custom_call" | custom-call | tf_op jit(solution)/shard_map/prepare/pallas_call | solution.py:182
  2.7 0.0 copy-start
  2.7 3.5 %collective-permute-start = (bf16[2064,128]{1,0:T(8,128)(2,1)}, bf16[2064,128]{1,0:T(8,128)(2,1)S(1)}, u32[]{:S(2)}, u32[]{:S(2)}) collective-permute-start(bf16[2064,128]{1,0:T(8,128)(2,1)} %prepare.1.a_ref), channel_id=1, source_target_pairs={{0,2},{1,3},{2,0},{3,1},{4,6},{5,7},{6,4},{7,5},{8,10},{9,11},{10,... | collective-permute-start | bytes 1585160 | tf_op jit(solution)/shard_map/ppermute | solution.py:246
  6.2 0.0 copy-done.2
  6.2 0.8 %broadcast_in_dim.2 = bf16[16,32,384]{2,1,0:T(8,128)(2,1)} broadcast(bf16[32,384]{1,0:T(8,128)(2,1)S(1)} %copy-done.2), dimensions={1,2} | broadcast | bytes 417792 | tf_op jit(solution)/shard_map/broadcast_in_dim | solution.py:242
  7.0 9.4 %all-to-all-start = ((bf16[16,32,384]{2,1,0:T(8,128)(2,1)}), bf16[16,32,384]{2,1,0:T(8,128)(2,1)S(1)}, u32[]{:S(2)}, u32[]{:S(2)}) async-start(bf16[16,32,384]{2,1,0:T(8,128)(2,1)} %broadcast_in_dim.2), calls=%async_computation | async-start | bytes 786432 | tf_op jit(solution)/shard_map/all_to_all | solution.py:244
  16.4 0.0 copy-done
  16.4 1.9 %collective-permute-start.1 = (bf16[2064,128]{1,0:T(8,128)(2,1)S(1)}, bf16[2064,128]{1,0:T(8,128)(2,1)S(1)}, u32[]{:S(2)}, u32[]{:S(2)}) collective-permute-start(bf16[2064,128]{1,0:T(8,128)(2,1)S(1)} %copy-done), channel_id=1, source_target_pairs={{0,1},{1,0},{2,3},{3,2},{4,5},{5,4},{6,7},{7,6},{8,9},{9,8},{10,11... | collective-permute-start | bytes 1585160 | tf_op jit(solution)/shard_map/ppermute | solution.py:247
  18.3 0.6 collective-permute-done.b_ref
  18.9 1.9 %collective-permute-start.2 = (bf16[2064,128]{1,0:T(8,128)(2,1)S(1)}, bf16[2064,128]{1,0:T(8,128)(2,1)S(1)}, u32[]{:S(2)}, u32[]{:S(2)}) collective-permute-start(bf16[2064,128]{1,0:T(8,128)(2,1)S(1)} %collective-permute-done.b_ref), channel_id=1, source_target_pairs={{0,1},{1,0},{2,3},{3,2},{4,5},{5,4},{6,7},{7,6},{8,9},{9,8},{10,11... | collective-permute-start | bytes 1585160 | tf_op jit(solution)/shard_map/ppermute | solution.py:248
  20.9 0.7 %pad_add_fusion.index_ref = s32[2]{0:T(128)} fusion(s32[1]{0:T(128)} %bitcast.5, s32[1]{0:T(128)} %bitcast.4), kind=kLoop, calls=%fused_computation | loop fusion | flops 2 | bytes 16 | tf_op jit(solution)/shard_map/stack | solution.py:238
  21.5 1.6 %bias.1.bias_ref = f32[512,128]{1,0:T(8,128)} custom-call(s32[2]{0:T(128)} %pad_add_fusion.index_ref, s32[512]{0:T(512)} %pos_smem.1, s32[4,128]{1,0:T(4,128)} %bitcast.9), custom_call_target="tpu_custom_call" | custom-call | tf_op jit(solution)/shard_map/bias/pallas_call | solution.py:192
  23.1 0.0 collective-permute-done.1.c_ref
  23.1 9.1 %all-to-all-done.q_ref = bf16[16,32,384]{2,1,0:T(8,128)(2,1)S(1)} async-done(((bf16[16,32,384]{2,1,0:T(8,128)(2,1)}), bf16[16,32,384]{2,1,0:T(8,128)(2,1)S(1)}, u32[]{:S(2)}, u32[]{:S(2)}) %all-to-all-start) | async-done | bytes 393248 | tf_op jit(solution)/shard_map/all_to_all | solution.py:244
  32.2 0.0 collective-permute-done.2.d_ref
  32.2 0.0 copy-start.1
  32.2 0.9 %copy-done.1 = f32[512,128]{1,0:T(8,128)S(1)} copy-done((f32[512,128]{1,0:T(8,128)S(1)}, f32[512,128]{1,0:T(8,128)}, u32[]{:S(2)}) %copy-start.1) | copy-done | bytes 262168
  33.2 8.2 %attend.1 = bf16[16,112,128]{2,1,0:T(8,128)(2,1)S(1)} custom-call(s32[1]{0:T(128)S(6)} %copy.8.fill_ref, bf16[16,32,384]{2,1,0:T(8,128)(2,1)S(1)} %all-to-all-done.q_ref, bf16[2064,128]{1,0:T(8,128)(2,1)S(1)} %copy-done, bf16[2064,128]{1,0:T(8,128)(2,1)S(1)} %collective-permute-done.b_ref, bf16[2064,128]{1,0:T(8,128)(2,1)S(1)} %collective-permute-done.1.c_ref, ...), custom_call_target="tpu_custom_call" | custom-call | flops 3221225472 | bytes 4194304 | tf_op jit(solution)/shard_map/attend/pallas_call | solution.py:206
  41.4 19.1 %all_to_all.10.part_ref = bf16[16,112,128]{2,1,0:T(8,128)(2,1)} all-to-all(bf16[16,112,128]{2,1,0:T(8,128)(2,1)S(1)} %attend.1), channel_id=1, replica_groups=mesh['ctx'=16,'head'=32] {'ctx'}, dimensions={0} | all-to-all | bytes 917504 | tf_op jit(solution)/shard_map/all_to_all | solution.py:251
  60.5 2.1 %combine.1 = bf16[32,384]{1,0:T(8,128)(2,1)} custom-call(bf16[16,112,128]{2,1,0:T(8,128)(2,1)} %all_to_all.10.part_ref), custom_call_target="tpu_custom_call" | custom-call | tf_op jit(solution)/shard_map/combine/pallas_call | solution.py:222
Async XLA Ops:
  0.7 5.6 %copy-start.2 = (bf16[32,384]{1,0:T(8,128)(2,1)S(1)}, bf16[32,384]{1,0:T(8,128)(2,1)}, u32[]{:S(2)}) copy-start(bf16[32,384]{1,0:T(8,128)(2,1)} %param.7) | copy-start | bytes 73732
  2.7 13.7 %copy-start = (bf16[2064,128]{1,0:T(8,128)(2,1)S(1)}, bf16[2064,128]{1,0:T(8,128)(2,1)}, u32[]{:S(2)}) copy-start(bf16[2064,128]{1,0:T(8,128)(2,1)} %prepare.1.a_ref) | copy-start | bytes 1585156
  2.7 16.2 %collective-permute-start = (bf16[2064,128]{1,0:T(8,128)(2,1)}, bf16[2064,128]{1,0:T(8,128)(2,1)S(1)}, u32[]{:S(2)}, u32[]{:S(2)}) collective-permute-start(bf16[2064,128]{1,0:T(8,128)(2,1)} %prepare.1.a_ref), channel_id=1, source_target_pairs={{0,2},{1,3},{2,0},{3,1},{4,6},{5,7},{6,4},{7,5},{8,10},{9,11},{10,... | collective-permute-start | bytes 1585160 | tf_op jit(solution)/shard_map/ppermute | solution.py:246
  7.0 25.2 %all-to-all-start = ((bf16[16,32,384]{2,1,0:T(8,128)(2,1)}), bf16[16,32,384]{2,1,0:T(8,128)(2,1)S(1)}, u32[]{:S(2)}, u32[]{:S(2)}) async-start(bf16[16,32,384]{2,1,0:T(8,128)(2,1)} %broadcast_in_dim.2), calls=%async_computation | async-start | bytes 786432 | tf_op jit(solution)/shard_map/all_to_all | solution.py:244
  16.4 6.7 %collective-permute-start.1 = (bf16[2064,128]{1,0:T(8,128)(2,1)S(1)}, bf16[2064,128]{1,0:T(8,128)(2,1)S(1)}, u32[]{:S(2)}, u32[]{:S(2)}) collective-permute-start(bf16[2064,128]{1,0:T(8,128)(2,1)S(1)} %copy-done), channel_id=1, source_target_pairs={{0,1},{1,0},{2,3},{3,2},{4,5},{5,4},{6,7},{7,6},{8,9},{9,8},{10,11... | collective-permute-start | bytes 1585160 | tf_op jit(solution)/shard_map/ppermute | solution.py:247
  18.9 13.3 %collective-permute-start.2 = (bf16[2064,128]{1,0:T(8,128)(2,1)S(1)}, bf16[2064,128]{1,0:T(8,128)(2,1)S(1)}, u32[]{:S(2)}, u32[]{:S(2)}) collective-permute-start(bf16[2064,128]{1,0:T(8,128)(2,1)S(1)} %collective-permute-done.b_ref), channel_id=1, source_target_pairs={{0,1},{1,0},{2,3},{3,2},{4,5},{5,4},{6,7},{7,6},{8,9},{9,8},{10,11... | collective-permute-start | bytes 1585160 | tf_op jit(solution)/shard_map/ppermute | solution.py:248
  32.2 1.0 %copy-start.1 = (f32[512,128]{1,0:T(8,128)S(1)}, f32[512,128]{1,0:T(8,128)}, u32[]{:S(2)}) copy-start(f32[512,128]{1,0:T(8,128)} %bias.1.bias_ref) | copy-start | bytes 786436

commit v3 on v2

--- a/solution.py
+++ b/solution.py
@@ -16,23 +16,50 @@
 AHEAD = 3
 KERNEL_VMEM = 24 * 1024 * 1024
 STAT_ROWS = 16
+META_ROWS = 16
 
 VMEM = pl.BlockSpec(memory_space=pltpu.VMEM)
 SMEM = pl.BlockSpec(memory_space=pltpu.SMEM)
-
-
-def prepare_kernel(fill_ref, k_ref, v_ref, tk_ref, tv_ref, kv_ref):
+HBM = pl.BlockSpec(memory_space=pltpu.HBM)
+
+
+def prepare_kernel(
+    fill_ref, q_hbm, k_hbm, v_hbm, tk_hbm, tv_hbm, spread_ref, kv_ref, q_ref, k_ref, v_ref, turn_ref, sems
+):
     slots, width = k_ref.shape
-    turn = tk_ref.shape[0]
-    fill = fill_ref[0]
+    turn = tk_hbm.shape[0]
+    pairs = (
+        (k_hbm, k_ref),
+        (v_hbm, v_ref),
+        (q_hbm, q_ref),
+        (tk_hbm, turn_ref.at[0]),
+        (tv_hbm, turn_ref.at[1]),
+    )
+    moves = [pltpu.make_async_copy(src, dst, sems.at[n]) for n, (src, dst) in enumerate(pairs)]
+    for move in moves:
+        move.start()
+    fill = jnp.broadcast_to(fill_ref[...], (width, width))
+    moves[0].wait()
     first = jnp.broadcast_to(k_ref[0:1, :].astype(jnp.float32), (width, width))
+    row = lax.broadcasted_iota(jnp.int32, (width, width), 0)
     for at in range(0, slots, width):
-        ok = lax.broadcasted_iota(jnp.int32, (width, width), 0) + at < fill
-        keys = jnp.where(ok, k_ref[at : at + width, :].astype(jnp.float32), first)
+        keys = jnp.where(row + at < fill, k_ref[at : at + width, :].astype(jnp.float32), first)
         kv_ref[at : at + width, :] = keys.T.astype(jnp.bfloat16)
-        values = jnp.where(ok, v_ref[at : at + width, :].astype(jnp.float32), 0.0)
+    moves[1].wait()
+    for at in range(0, slots, width):
+        values = jnp.where(row + at < fill, v_ref[at : at + width, :].astype(jnp.float32), 0.0)
         kv_ref[slots + at : slots + at + width, :] = values.astype(jnp.bfloat16)
-    kv_ref[2 * slots : 2 * slots + 2 * turn, :] = jnp.concatenate([tk_ref[...], tv_ref[...]], axis=0)
+    moves[2].wait()
+    for at in range(spread_ref.shape[0]):
+        spread_ref[at] = q_ref[...]
+    moves[3].wait()
+    moves[4].wait()
+    at = 2 * slots
+    kv_ref[at : at + 2 * turn, :] = jnp.concatenate([turn_ref[0], turn_ref[1]], axis=0)
+    at += 2 * turn
+    half = lax.broadcasted_iota(jnp.int32, (META_ROWS, width), 0) < META_ROWS // 2
+    meta = jnp.where(half, fill[:META_ROWS] >> 5, fill[:META_ROWS] & 31)
+    kv_ref[at : at + META_ROWS, :] = meta.astype(jnp.float32).astype(jnp.bfloat16)
 
 
 def bias_kernel(index_ref, pos_smem, pos_ref, bias_ref):
@@ -40,10 +67,10 @@
     ctx, sub = index_ref[0], index_ref[1]
     lane = lax.broadcasted_iota(jnp.int32, (1, width), 1)
     keys = jnp.full((1, width), 1 << 20, jnp.int32)
-    for n, flip in enumerate((0, 2, 1, 3)):
-        base = (sub ^ flip) * width + ctx * 8
+    core = sub % 2
+    for n, (at, flip) in enumerate(((ctx, 0), (ctx, 1), (ctx ^ core, 2), (ctx ^ 1 ^ core, 3))):
         for i in range(8):
-            keys = jnp.where(lane == n * 8 + i, pos_smem[base + i], keys)
+            keys = jnp.where(lane == n * 8 + i, pos_smem[(sub ^ flip) * width + at * 8 + i], keys)
     keys = keys.astype(jnp.float32)
     pos = pos_ref[...].astype(jnp.float32)
     for b in range(blocks):
@@ -52,18 +79,17 @@
 
 
 def attend_kernel(
-    fill_ref, q_ref, a_ref, b_ref, c_ref, d_ref, bias_ref, out_ref, total_ref, peak_ref, *, slots, turn
+    q_ref, own_ref, near_ref, far_ref, diagonal_ref, bias_ref, out_ref, total_ref, peak_ref, *, slots, turn
 ):
-    sources = (a_ref, b_ref, c_ref, d_ref)
+    sources = (own_ref, near_ref, far_ref, diagonal_ref)
     blocks, tokens, columns = q_ref.shape
-    width = a_ref.shape[1]
+    width = own_ref.shape[1]
     heads = columns // width
     rows = heads * tokens
     size = TILE * rows
     tiles = blocks // TILE
     count = turn * len(sources)
     factor = math.log2(math.e) / math.sqrt(width)
-    fill = fill_ref[0]
     plain = (((1,), (0,)), ((), ()))
     contract = (((1,), (1,)), ((), ()))
 
@@ -72,6 +98,13 @@
 
     def weights(scores, peak):
         return jnp.exp2(scores * factor - peak).astype(jnp.bfloat16)
+
+    def visible(source, start):
+        meta = source[2 * slots + 2 * turn :, :].astype(jnp.float32)
+        half = META_ROWS // 2
+        fill = meta[0:1] * 32 + meta[half : half + 1]
+        slot = lax.broadcasted_iota(jnp.int32, (STEP, width), 0) + start
+        return jnp.where(slot.astype(jnp.float32) < fill, 1.0, 0.0).astype(jnp.bfloat16)
 
     def turned(index):
         pairs = [s[2 * slots : 2 * slots + 2 * turn, :] for s in sources]
@@ -100,12 +133,16 @@
             )
             out_ref[at, rows : rows + STAT_ROWS, :] = stat.astype(jnp.bfloat16)
 
-    def step(start, first, last):
-        keys = jnp.concatenate([s[start + b : start + b + width, :] for s in sources for b in range(0, STEP, width)], axis=1)
-        slot = lax.broadcasted_iota(jnp.int32, (STEP, width), 0) + start
-        flag = jnp.where(slot < fill, 1.0, 0.0).astype(jnp.bfloat16)
+    def step(start, taken, first, last):
+        keys = jnp.concatenate(
+            [s[start + b : start + b + width, :] for s in taken for b in range(0, STEP, width)], axis=1
+        )
         values = jnp.concatenate(
-            [jnp.concatenate([s[slots + start : slots + start + STEP, :], flag], axis=1) for s in sources], axis=0
+            [
+                jnp.concatenate([s[slots + start : slots + start + STEP, :], visible(s, start)], axis=1)
+                for s in taken
+            ],
+            axis=0,
         )
 
         def score(t):
@@ -149,14 +186,26 @@
         for waiting in ahead:
             mix(*waiting)
 
-    @pl.when(fill <= STEP)
-    def _():
-        step(0, True, True)
-
-    @pl.when(fill > STEP)
-    def _():
-        for start in range(0, slots, STEP):
-            step(start, start == 0, start + STEP == slots)
+    def more(source):
+        meta = source[2 * slots + 2 * turn :, :].astype(jnp.float32)
+        half = META_ROWS // 2
+        return jnp.max(meta[:half]) * 32 + jnp.max(meta[half:]) > STEP
+
+    wide = [more(s) for s in (own_ref, far_ref, diagonal_ref)]
+    step(0, sources, True, False)
+
+    for mine, first, second in ((0, 0, 0), (0, 0, 1), (0, 1, 0), (1, 0, 1), (1, 1, 0), (1, 1, 1)):
+        rest = sources[:2] * mine + sources[2:3] * first + sources[3:] * second
+        given = [w if want else jnp.logical_not(w) for w, want in zip(wide, (mine, first, second))]
+
+        @pl.when(given[0] & given[1] & given[2])
+        def _(rest=rest):
+            if rest:
+                step(STEP, rest, False, True)
+            else:
+                for t in range(tiles):
+                    at = slice(t * size, (t + 1) * size)
+                    finish(t, total_ref[at, :], peak_ref[at, :])
 
 
 def combine_kernel(part_ref, out_ref):
@@ -177,15 +226,27 @@
         out_ref[:, h * width : (h + 1) * width] = total[h * tokens : (h + 1) * tokens]
 
 
-def prepare(fill, keys, values, turn_k, turn_v):
+def prepare(fill, queries, keys, values, turn_k, turn_v, copies):
     slots, width = keys.shape
+    turn = turn_k.shape[0]
     return pl.pallas_call(
         prepare_kernel,
-        out_shape=jax.ShapeDtypeStruct((2 * slots + 2 * turn_k.shape[0], width), jnp.bfloat16),
-        in_specs=[SMEM] + [VMEM] * 4,
-        out_specs=VMEM,
+        out_shape=[
+            jax.ShapeDtypeStruct((copies, *queries.shape), jnp.bfloat16),
+            jax.ShapeDtypeStruct((2 * slots + 2 * turn + META_ROWS, width), jnp.bfloat16),
+        ],
+        in_specs=[VMEM] + [HBM] * 5,
+        out_specs=[VMEM, VMEM],
+        scratch_shapes=[
+            pltpu.VMEM(queries.shape, jnp.bfloat16),
+            pltpu.VMEM(keys.shape, jnp.bfloat16),
+            pltpu.VMEM(values.shape, jnp.bfloat16),
+            pltpu.VMEM((2, turn, width), jnp.bfloat16),
+            pltpu.SemaphoreType.DMA((5,)),
+        ],
+        compiler_params=pltpu.CompilerParams(vmem_limit_bytes=56 * 1024 * 1024),
         name="prepare",
-    )(fill, keys, values, turn_k, turn_v)
+    )(fill.reshape(1, 1), queries, keys, values, turn_k, turn_v)
 
 
 def bias_of(index, positions, width):
@@ -194,19 +255,20 @@
         out_shape=jax.ShapeDtypeStruct((positions.shape[0], width), jnp.float32),
         in_specs=[SMEM, SMEM, VMEM],
         out_specs=VMEM,
+        compiler_params=pltpu.CompilerParams(vmem_limit_bytes=4 * 1024 * 1024),
         name="bias",
     )(index, positions, positions.reshape(-1, width))
 
 
-def attend(fill, q, sources, bias, slots, turn):
+def attend(q, sources, bias, slots, turn):
     blocks, tokens, columns = q.shape
-    width = bias.shape[1]
+    width = sources[0].shape[1]
     rows = tokens * columns // width
     work = blocks * rows * slots * len(sources)
     return pl.pallas_call(
         functools.partial(attend_kernel, slots=slots, turn=turn),
         out_shape=jax.ShapeDtypeStruct((blocks, rows + STAT_ROWS, width), jnp.bfloat16),
-        in_specs=[SMEM] + [VMEM] * 6,
+        in_specs=[VMEM] * 6,
         out_specs=VMEM,
         scratch_shapes=[
             pltpu.VMEM((blocks * rows, 2 * width), jnp.float32),
@@ -215,7 +277,7 @@
         compiler_params=pltpu.CompilerParams(vmem_limit_bytes=KERNEL_VMEM),
         cost_estimate=pl.CostEstimate(flops=4 * work * width, bytes_accessed=4 << 20, transcendentals=work),
         name="attend",
-    )(fill, q, *sources, bias)
+    )(q, *sources, bias)
 
 
 def combine(parts, tokens, columns):
@@ -224,6 +286,7 @@
         out_shape=jax.ShapeDtypeStruct((tokens, columns), jnp.bfloat16),
         in_specs=[VMEM],
         out_specs=VMEM,
+        compiler_params=pltpu.CompilerParams(vmem_limit_bytes=4 * 1024 * 1024),
         name="combine",
     )(parts)
 
@@ -236,18 +299,20 @@
     n_ctx, n_head = lax.axis_size("ctx"), lax.axis_size("head")
     sub = lax.axis_index("head") % (n_head // KV_HEADS)
     index = jnp.stack([lax.axis_index("ctx"), sub]).astype(jnp.int32)
-    other = [(i, i ^ 1) for i in range(n_head)]
-    across = [(i, i ^ 2) for i in range(n_head)]
-
-    copies = jnp.broadcast_to(queries[None], (n_ctx, tokens, columns))
-    copies, cache_fill = lax.optimization_barrier((copies, cache_fill))
+    other = [(h, h ^ 1) for h in range(n_head)]
+    across = [
+        (c * n_head + h, (c ^ (h & 1)) * n_head + (h ^ 2)) for c in range(n_ctx) for h in range(n_head)
+    ]
+
+    copies, own = prepare(
+        cache_fill, queries, cache_keys[0], cache_values[0], turn_keys[0], turn_values[0], n_ctx
+    )
     q = lax.all_to_all(copies, "ctx", split_axis=0, concat_axis=0, tiled=True)
-    own = prepare(cache_fill, cache_keys[0], cache_values[0], turn_keys[0], turn_values[0])
-    far = lax.ppermute(own, "head", across)
+    far = lax.ppermute(own, ("ctx", "head"), across)
     near = lax.ppermute(own, "head", other)
     diagonal = lax.ppermute(far, "head", other)
     bias = bias_of(index, turn_positions, width)
-    parts = attend(cache_fill, q, (own, far, near, diagonal), bias, slots, turn)
+    parts = attend(q, (own, near, far, diagonal), bias, slots, turn)
     parts = lax.all_to_all(parts, "ctx", split_axis=0, concat_axis=0, tiled=True)
     return combine(parts, tokens, columns)
 

time: 63 us -> 58.7 us (0.932)
  Pallas kernels: 13.9 us -> 11.6 us
  local copies, waits for them, and re-layouts: 1.74 us -> 0.6 us
    pallas_call x1, Pallas kernels: 2.08 us -> 1.07 us  [combine(): pl.pallas_call(combine_kernel, out_shape=jax.ShapeDtypeStruct((tokens, co...]
    pallas_call x1, Pallas kernels: 1.56 us -> 0.7 us  [bias_of(): pl.pallas_call(bias_kernel, out_shape=jax.ShapeDtypeStruct((positions.sha...]
    broadcast_in_dim x1 -> x0, local copies, waits for them, and re-layouts: 0.78 us -> none  [body(): copies = jnp.broadcast_to(queries[None], (n_ctx, tokens, columns))]
  transfers between devices with their start and end apart: 4 -> 4, of which waited for: 2 -> 1; matrix products, arithmetic and copies ran while one was open for 2% -> 0% of each run, Pallas kernels for 2% -> 1%
where the time goes in v3:
time: 58.7 us; the launch traced here: 58.8 us
  blocking collectives  19 us (32%)
  starting transfers between devices  17.2 us (29%)
  Pallas kernels  11.6 us (20%)
  waiting for transfers between devices  9.49 us (16%)
  between operations  0.76 us (1%)
  local copies, waits for them, and re-layouts  0.6 us (1%)
    all_to_all x1, blocking collectives, body(): lax.all_to_all(parts, 'ctx', split_axis=0, concat_axis=0, tiled=True)  19 us
    all_to_all x1, waiting for transfers between devices, body(): q = lax.all_to_all(copies, 'ctx', split_axis=0, concat_axis=0, tiled=True)  9.48 us
    all_to_all x1, starting transfers between devices, body(): q = lax.all_to_all(copies, 'ctx', split_axis=0, concat_axis=0, tiled=True)  9.38 us
    pallas_call x1, Pallas kernels, attend(): pl.pallas_call(functools.partial(attend_kernel, slots=slots, turn=turn),...  7.68 us
    ppermute x1, starting transfers between devices, body(): far = lax.ppermute(own, ('ctx', 'head'), across)  3.53 us
    ppermute x1, starting transfers between devices, body(): diagonal = lax.ppermute(far, 'head', other)  2.41 us
    pallas_call x1, Pallas kernels, prepare(): pl.pallas_call(prepare_kernel, out_shape=[jax.ShapeDtypeStruct((copies, *...  2.2 us
    ppermute x1, starting transfers between devices, body(): near = lax.ppermute(own, 'head', other)  1.92 us
  transfers between devices with their start and end apart: 4, of which 1 were waited for; matrix products, arithmetic and copies ran while one was open for 0% of the time, Pallas kernels for 1%

profile of v3, /device:TPU:448, one launch (start us, length us, event | category | flops | bytes accessed | tf_op | source)
XLA Modules:
  0.0 58.8 jit_solution(2116818801052242817)
XLA Ops:
  0.7 2.2 %prepare.1 = (bf16[16,32,384]{2,1,0:T(8,128)(2,1)}, bf16[2080,128]{1,0:T(8,128)(2,1)}) custom-call(s32[1,1]{1,0:T(1,128)} %bitcast.8.fill_ref, bf16[32,384]{1,0:T(8,128)(2,1)} %q_hbm.1, bf16[1024,128]{1,0:T(8,128)(2,1)} %bitcast.10, bf16[1024,128]{1,0:T(8,128)(2,1)} %bitcast.11, bf16[8,128]{1,0:T(8,128)(2,1)} %bitcast.12, bf16[8,128]{1,0:T(8,128)(2,1)} %bitcast.13), custom_call_target="tpu_custom_call" | custom-call | tf_op jit(solution)/shard_map/prepare/pallas_call | solution.py:232
  2.9 0.0 copy-start.1
  2.9 3.5 %collective-permute-start.1 = (bf16[2080,128]{1,0:T(8,128)(2,1)}, bf16[2080,128]{1,0:T(8,128)(2,1)S(1)}, u32[]{:S(2)}, u32[]{:S(2)}) collective-permute-start(bf16[2080,128]{1,0:T(8,128)(2,1)} %get-tuple-element.8.own_ref), channel_id=1, source_target_pairs={{0,2},{1,35},{2,0},{3,33},{4,6},{5,39},{6,4},{7,37},{8,10},{9,43},... | collective-permute-start | bytes 1597448 | tf_op jit(solution)/shard_map/ppermute | solution.py:311
  6.4 9.4 %all-to-all-start = ((bf16[16,32,384]{2,1,0:T(8,128)(2,1)}), bf16[16,32,384]{2,1,0:T(8,128)(2,1)S(1)}, u32[]{:S(2)}, u32[]{:S(2)}) async-start(bf16[16,32,384]{2,1,0:T(8,128)(2,1)} %get-tuple-element.7), calls=%async_computation | async-start | bytes 786432 | tf_op jit(solution)/shard_map/all_to_all | solution.py:310
  15.8 0.0 copy-done.1
  15.8 1.9 %collective-permute-start = (bf16[2080,128]{1,0:T(8,128)(2,1)S(1)}, bf16[2080,128]{1,0:T(8,128)(2,1)S(1)}, u32[]{:S(2)}, u32[]{:S(2)}) collective-permute-start(bf16[2080,128]{1,0:T(8,128)(2,1)S(1)} %copy-done.1), channel_id=1, source_target_pairs={{0,1},{1,0},{2,3},{3,2},{4,5},{5,4},{6,7},{7,6},{8,9},{9,8},{10,11... | collective-permute-start | bytes 1597448 | tf_op jit(solution)/shard_map/ppermute | solution.py:312
  17.7 0.0 collective-permute-done.1.far_ref
  17.8 2.4 %collective-permute-start.2 = (bf16[2080,128]{1,0:T(8,128)(2,1)S(1)}, bf16[2080,128]{1,0:T(8,128)(2,1)S(1)}, u32[]{:S(2)}, u32[]{:S(2)}) collective-permute-start(bf16[2080,128]{1,0:T(8,128)(2,1)S(1)} %collective-permute-done.1.far_ref), channel_id=1, source_target_pairs={{0,1},{1,0},{2,3},{3,2},{4,5},{5,4},{6,7},{7,6},{8,9},{9,8},{10,11... | collective-permute-start | bytes 1597448 | tf_op jit(solution)/shard_map/ppermute | solution.py:313
  20.2 0.0 copy-start
  20.2 0.1 pad_add_fusion.index_ref
  20.3 0.6 %copy-done = s32[512]{0:T(512)S(1)} copy-done((s32[512]{0:T(512)S(1)}, s32[512]{0:T(512)}, u32[]{:S(2)}) %copy-start) | copy-done | bytes 2072
  20.9 0.7 %bias.1.bias_ref = f32[512,128]{1,0:T(8,128)S(1)} custom-call(s32[2]{0:T(128)S(1)} %pad_add_fusion.index_ref, s32[512]{0:T(512)S(1)} %copy-done, s32[4,128]{1,0:T(4,128)S(1)} %bitcast.9), custom_call_target="tpu_custom_call" | custom-call | tf_op jit(solution)/shard_map/bias/pallas_call | solution.py:253
  21.6 0.0 collective-permute-done.near_ref
  21.6 9.5 %all-to-all-done.q_ref = bf16[16,32,384]{2,1,0:T(8,128)(2,1)S(1)} async-done(((bf16[16,32,384]{2,1,0:T(8,128)(2,1)}), bf16[16,32,384]{2,1,0:T(8,128)(2,1)S(1)}, u32[]{:S(2)}, u32[]{:S(2)}) %all-to-all-start) | async-done | bytes 393248 | tf_op jit(solution)/shard_map/all_to_all | solution.py:310
  31.1 0.0 collective-permute-done.2.diagonal_ref
  31.1 7.7 %attend.1 = bf16[16,112,128]{2,1,0:T(8,128)(2,1)S(1)} custom-call(bf16[16,32,384]{2,1,0:T(8,128)(2,1)S(1)} %all-to-all-done.q_ref, bf16[2080,128]{1,0:T(8,128)(2,1)S(1)} %copy-done.1, bf16[2080,128]{1,0:T(8,128)(2,1)S(1)} %collective-permute-done.near_ref, bf16[2080,128]{1,0:T(8,128)(2,1)S(1)} %collective-permute-done.1.far_ref, ...), custom_call_target="tpu_custom_call" | custom-call | flops 3221225472 | bytes 4194304 | tf_op jit(solution)/shard_map/attend/pallas_call | solution.py:268
  38.8 19.0 %all_to_all.10.part_ref = bf16[16,112,128]{2,1,0:T(8,128)(2,1)S(1)} all-to-all(bf16[16,112,128]{2,1,0:T(8,128)(2,1)S(1)} %attend.1), channel_id=1, replica_groups=mesh['ctx'=16,'head'=32] {'ctx'}, dimensions={0} | all-to-all | bytes 917504 | tf_op jit(solution)/shard_map/all_to_all | solution.py:316
  57.7 1.1 %combine.1 = bf16[32,384]{1,0:T(8,128)(2,1)} custom-call(bf16[16,112,128]{2,1,0:T(8,128)(2,1)S(1)} %all_to_all.10.part_ref), custom_call_target="tpu_custom_call" | custom-call | tf_op jit(solution)/shard_map/combine/pallas_call | solution.py:284
Async XLA Ops:
  2.9 12.9 %copy-start.1 = (bf16[2080,128]{1,0:T(8,128)(2,1)S(1)}, bf16[2080,128]{1,0:T(8,128)(2,1)}, u32[]{:S(2)}) copy-start(bf16[2080,128]{1,0:T(8,128)(2,1)} %get-tuple-element.8.own_ref) | copy-start | bytes 1597444
  2.9 14.9 %collective-permute-start.1 = (bf16[2080,128]{1,0:T(8,128)(2,1)}, bf16[2080,128]{1,0:T(8,128)(2,1)S(1)}, u32[]{:S(2)}, u32[]{:S(2)}) collective-permute-start(bf16[2080,128]{1,0:T(8,128)(2,1)} %get-tuple-element.8.own_ref), channel_id=1, source_target_pairs={{0,2},{1,35},{2,0},{3,33},{4,6},{5,39},{6,4},{7,37},{8,10},{9,43},... | collective-permute-start | bytes 1597448 | tf_op jit(solution)/shard_map/ppermute | solution.py:311
  6.4 24.7 %all-to-all-start = ((bf16[16,32,384]{2,1,0:T(8,128)(2,1)}), bf16[16,32,384]{2,1,0:T(8,128)(2,1)S(1)}, u32[]{:S(2)}, u32[]{:S(2)}) async-start(bf16[16,32,384]{2,1,0:T(8,128)(2,1)} %get-tuple-element.7), calls=%async_computation | async-start | bytes 786432 | tf_op jit(solution)/shard_map/all_to_all | solution.py:310
  15.8 5.8 %collective-permute-start = (bf16[2080,128]{1,0:T(8,128)(2,1)S(1)}, bf16[2080,128]{1,0:T(8,128)(2,1)S(1)}, u32[]{:S(2)}, u32[]{:S(2)}) collective-permute-start(bf16[2080,128]{1,0:T(8,128)(2,1)S(1)} %copy-done.1), channel_id=1, source_target_pairs={{0,1},{1,0},{2,3},{3,2},{4,5},{5,4},{6,7},{7,6},{8,9},{9,8},{10,11... | collective-permute-start | bytes 1597448 | tf_op jit(solution)/shard_map/ppermute | solution.py:312
  17.8 13.3 %collective-permute-start.2 = (bf16[2080,128]{1,0:T(8,128)(2,1)S(1)}, bf16[2080,128]{1,0:T(8,128)(2,1)S(1)}, u32[]{:S(2)}, u32[]{:S(2)}) collective-permute-start(bf16[2080,128]{1,0:T(8,128)(2,1)S(1)} %collective-permute-done.1.far_ref), channel_id=1, source_target_pairs={{0,1},{1,0},{2,3},{3,2},{4,5},{5,4},{6,7},{7,6},{8,9},{9,8},{10,11... | collective-permute-start | bytes 1597448 | tf_op jit(solution)/shard_map/ppermute | solution.py:313
  20.2 0.7 %copy-start = (s32[512]{0:T(512)S(1)}, s32[512]{0:T(512)}, u32[]{:S(2)}) copy-start(s32[512]{0:T(512)} %pos_smem.1) | copy-start | bytes 6148

commit v4 on v3

--- a/solution.py
+++ b/solution.py
@@ -24,11 +24,30 @@
 
 
 def prepare_kernel(
-    fill_ref, q_hbm, k_hbm, v_hbm, tk_hbm, tv_hbm, spread_ref, kv_ref, q_ref, k_ref, v_ref, turn_ref, sems
+    fill_ref,
+    place_hbm,
+    pos_hbm,
+    q_hbm,
+    k_hbm,
+    v_hbm,
+    tk_hbm,
+    tv_hbm,
+    spread_ref,
+    kv_ref,
+    bias_ref,
+    place_ref,
+    pos_ref,
+    q_ref,
+    k_ref,
+    v_ref,
+    turn_ref,
+    sems,
 ):
     slots, width = k_ref.shape
     turn = tk_hbm.shape[0]
     pairs = (
+        (place_hbm, place_ref),
+        (pos_hbm, pos_ref),
         (k_hbm, k_ref),
         (v_hbm, v_ref),
         (q_hbm, q_ref),
@@ -38,22 +57,40 @@
     moves = [pltpu.make_async_copy(src, dst, sems.at[n]) for n, (src, dst) in enumerate(pairs)]
     for move in moves:
         move.start()
+    ctx = lax.axis_index("ctx")
+    sub = lax.axis_index("head") % (lax.axis_size("head") // KV_HEADS)
+    core = sub % 2
+    moves[0].wait()
+    lane = lax.broadcasted_iota(jnp.int32, (1, width), 1)
+    seat = jnp.full((1, width), 1 << 20, jnp.int32)
+    for n, (at, flip) in enumerate(((ctx, 0), (ctx, 1), (ctx ^ core, 2), (ctx ^ 1 ^ core, 3))):
+        for i in range(turn):
+            seat = jnp.where(lane == n * turn + i, place_ref[(sub ^ flip) * width + at * turn + i], seat)
+    seat = seat.astype(jnp.float32)
+    moves[1].wait()
+    pos = pos_ref[...].astype(jnp.float32)
+    for b in range(pos.shape[0]):
+        tokens = jnp.broadcast_to(pos[b : b + 1, :], (width, width)).T
+        bias_ref[b * width : (b + 1) * width, :] = jnp.where(seat <= tokens, 0.0, NEGATIVE).astype(jnp.bfloat16)
     fill = jnp.broadcast_to(fill_ref[...], (width, width))
-    moves[0].wait()
+    moves[2].wait()
     first = jnp.broadcast_to(k_ref[0:1, :].astype(jnp.float32), (width, width))
     row = lax.broadcasted_iota(jnp.int32, (width, width), 0)
     for at in range(0, slots, width):
         keys = jnp.where(row + at < fill, k_ref[at : at + width, :].astype(jnp.float32), first)
         kv_ref[at : at + width, :] = keys.T.astype(jnp.bfloat16)
-    moves[1].wait()
+    moves[3].wait()
     for at in range(0, slots, width):
         values = jnp.where(row + at < fill, v_ref[at : at + width, :].astype(jnp.float32), 0.0)
         kv_ref[slots + at : slots + at + width, :] = values.astype(jnp.bfloat16)
-    moves[2].wait()
-    for at in range(spread_ref.shape[0]):
-        spread_ref[at] = q_ref[...]
-    moves[3].wait()
     moves[4].wait()
+    tokens, columns = q_ref.shape
+    for h in range(columns // width):
+        own_q = q_ref[:, h * width : (h + 1) * width]
+        for at in range(spread_ref.shape[0]):
+            spread_ref[at, h * tokens : (h + 1) * tokens, :] = own_q
+    moves[5].wait()
+    moves[6].wait()
     at = 2 * slots
     kv_ref[at : at + 2 * turn, :] = jnp.concatenate([turn_ref[0], turn_ref[1]], axis=0)
     at += 2 * turn
@@ -62,30 +99,13 @@
     kv_ref[at : at + META_ROWS, :] = meta.astype(jnp.float32).astype(jnp.bfloat16)
 
 
-def bias_kernel(index_ref, pos_smem, pos_ref, bias_ref):
-    blocks, width = pos_ref.shape
-    ctx, sub = index_ref[0], index_ref[1]
-    lane = lax.broadcasted_iota(jnp.int32, (1, width), 1)
-    keys = jnp.full((1, width), 1 << 20, jnp.int32)
-    core = sub % 2
-    for n, (at, flip) in enumerate(((ctx, 0), (ctx, 1), (ctx ^ core, 2), (ctx ^ 1 ^ core, 3))):
-        for i in range(8):
-            keys = jnp.where(lane == n * 8 + i, pos_smem[(sub ^ flip) * width + at * 8 + i], keys)
-    keys = keys.astype(jnp.float32)
-    pos = pos_ref[...].astype(jnp.float32)
-    for b in range(blocks):
-        tokens = jnp.broadcast_to(pos[b : b + 1, :], (width, width)).T
-        bias_ref[b * width : (b + 1) * width, :] = jnp.where(keys <= tokens, 0.0, NEGATIVE)
-
-
 def attend_kernel(
     q_ref, own_ref, near_ref, far_ref, diagonal_ref, bias_ref, out_ref, total_ref, peak_ref, *, slots, turn
 ):
     sources = (own_ref, near_ref, far_ref, diagonal_ref)
-    blocks, tokens, columns = q_ref.shape
-    width = own_ref.shape[1]
-    heads = columns // width
-    rows = heads * tokens
+    blocks, rows, width = q_ref.shape
+    tokens = bias_ref.shape[0] // blocks
+    heads = rows // tokens
     size = TILE * rows
     tiles = blocks // TILE
     count = turn * len(sources)
@@ -146,15 +166,12 @@
         )
 
         def score(t):
-            q = jnp.concatenate(
-                [q_ref[t * TILE + n, :, h * width : (h + 1) * width] for n in range(TILE) for h in range(heads)],
-                axis=0,
-            )
+            q = jnp.concatenate([q_ref[t * TILE + n] for n in range(TILE)], axis=0)
             if not first:
                 return dot(q, keys), None
             bias = jnp.concatenate(
                 [
-                    bias_ref[(t * TILE + n) * tokens : (t * TILE + n + 1) * tokens, 0:count]
+                    bias_ref[(t * TILE + n) * tokens : (t * TILE + n + 1) * tokens, :].astype(jnp.float32)[:, 0:count]
                     for n in range(TILE)
                     for h in range(heads)
                 ],
@@ -226,44 +243,35 @@
         out_ref[:, h * width : (h + 1) * width] = total[h * tokens : (h + 1) * tokens]
 
 
-def prepare(fill, queries, keys, values, turn_k, turn_v, copies):
+def prepare(fill, positions, queries, keys, values, turn_k, turn_v, copies):
     slots, width = keys.shape
+    seats = (positions.shape[0] // width, width)
     turn = turn_k.shape[0]
     return pl.pallas_call(
         prepare_kernel,
         out_shape=[
-            jax.ShapeDtypeStruct((copies, *queries.shape), jnp.bfloat16),
+            jax.ShapeDtypeStruct((copies, queries.size // width, width), jnp.bfloat16),
             jax.ShapeDtypeStruct((2 * slots + 2 * turn + META_ROWS, width), jnp.bfloat16),
+            jax.ShapeDtypeStruct((positions.shape[0], width), jnp.bfloat16),
         ],
-        in_specs=[VMEM] + [HBM] * 5,
-        out_specs=[VMEM, VMEM],
+        in_specs=[VMEM] + [HBM] * 7,
+        out_specs=[VMEM] * 3,
         scratch_shapes=[
+            pltpu.SMEM(positions.shape, jnp.int32),
+            pltpu.VMEM(seats, jnp.int32),
             pltpu.VMEM(queries.shape, jnp.bfloat16),
             pltpu.VMEM(keys.shape, jnp.bfloat16),
             pltpu.VMEM(values.shape, jnp.bfloat16),
             pltpu.VMEM((2, turn, width), jnp.bfloat16),
-            pltpu.SemaphoreType.DMA((5,)),
+            pltpu.SemaphoreType.DMA((7,)),
         ],
         compiler_params=pltpu.CompilerParams(vmem_limit_bytes=56 * 1024 * 1024),
         name="prepare",
-    )(fill.reshape(1, 1), queries, keys, values, turn_k, turn_v)
-
-
-def bias_of(index, positions, width):
-    return pl.pallas_call(
-        bias_kernel,
-        out_shape=jax.ShapeDtypeStruct((positions.shape[0], width), jnp.float32),
-        in_specs=[SMEM, SMEM, VMEM],
-        out_specs=VMEM,
-        compiler_params=pltpu.CompilerParams(vmem_limit_bytes=4 * 1024 * 1024),
-        name="bias",
-    )(index, positions, positions.reshape(-1, width))
+    )(fill.reshape(1, 1), positions, positions.reshape(seats), queries, keys, values, turn_k, turn_v)
 
 
 def attend(q, sources, bias, slots, turn):
-    blocks, tokens, columns = q.shape
-    width = sources[0].shape[1]
-    rows = tokens * columns // width
+    blocks, rows, width = q.shape
     work = blocks * rows * slots * len(sources)
     return pl.pallas_call(
         functools.partial(attend_kernel, slots=slots, turn=turn),
@@ -297,21 +305,18 @@
     slots = cache_keys.shape[1]
     turn = turn_keys.shape[1]
     n_ctx, n_head = lax.axis_size("ctx"), lax.axis_size("head")
-    sub = lax.axis_index("head") % (n_head // KV_HEADS)
-    index = jnp.stack([lax.axis_index("ctx"), sub]).astype(jnp.int32)
     other = [(h, h ^ 1) for h in range(n_head)]
     across = [
         (c * n_head + h, (c ^ (h & 1)) * n_head + (h ^ 2)) for c in range(n_ctx) for h in range(n_head)
     ]
 
-    copies, own = prepare(
-        cache_fill, queries, cache_keys[0], cache_values[0], turn_keys[0], turn_values[0], n_ctx
+    copies, own, bias = prepare(
+        cache_fill, turn_positions, queries, cache_keys[0], cache_values[0], turn_keys[0], turn_values[0], n_ctx
     )
     q = lax.all_to_all(copies, "ctx", split_axis=0, concat_axis=0, tiled=True)
     far = lax.ppermute(own, ("ctx", "head"), across)
     near = lax.ppermute(own, "head", other)
     diagonal = lax.ppermute(far, "head", other)
-    bias = bias_of(index, turn_positions, width)
     parts = attend(q, (own, near, far, diagonal), bias, slots, turn)
     parts = lax.all_to_all(parts, "ctx", split_axis=0, concat_axis=0, tiled=True)
     return combine(parts, tokens, columns)

time: 58.7 us -> 59 us (level); the launches traced: 58.8 us -> 58.4 us
  waiting for transfers between devices: 9.49 us -> 10.9 us
  Pallas kernels: 11.6 us -> 10.2 us
  local copies, waits for them, and re-layouts: 0.6 us -> 0.01 us
    all_to_all x1, waiting for transfers between devices: 9.48 us -> 10.9 us  [body(): q = lax.all_to_all(copies, 'ctx', split_axis=0, concat_axis=0, tiled=True)]
    pallas_call x1, Pallas kernels: 7.68 us -> 6.85 us  [attend(): pl.pallas_call(functools.partial(attend_kernel, slots=slots, turn=turn),...]
    pallas_call x2 -> x1, Pallas kernels: 2.9 us -> 2.28 us  [prepare(): pl.pallas_call(prepare_kernel, out_shape=[jax.ShapeDtypeStruct((copies, q...]
    unnamed x4, local copies, waits for them, and re-layouts: 0.6 us -> 0.01 us
  transfers between devices with their start and end apart: 4 -> 4, of which waited for: 1 -> 1; matrix products, arithmetic and copies ran while one was open for 0% -> 0% of each run, Pallas kernels for 1% -> 0%
where the time goes in v4:
time: 59 us; the launch traced here: 58.4 us
  blocking collectives  19.2 us (33%)
  starting transfers between devices  17.4 us (29%)
  waiting for transfers between devices  10.9 us (18%)
  Pallas kernels  10.2 us (17%)
  between operations  0.74 us (1%)
    all_to_all x1, blocking collectives, body(): lax.all_to_all(parts, 'ctx', split_axis=0, concat_axis=0, tiled=True)  19.2 us
    all_to_all x1, waiting for transfers between devices, body(): q = lax.all_to_all(copies, 'ctx', split_axis=0, concat_axis=0, tiled=True)  10.9 us
    all_to_all x1, starting transfers between devices, body(): q = lax.all_to_all(copies, 'ctx', split_axis=0, concat_axis=0, tiled=True)  9.52 us
    pallas_call x1, Pallas kernels, attend(): pl.pallas_call(functools.partial(attend_kernel, slots=slots, turn=turn),...  6.85 us
    ppermute x1, starting transfers between devices, body(): far = lax.ppermute(own, ('ctx', 'head'), across)  3.53 us
    ppermute x1, starting transfers between devices, body(): diagonal = lax.ppermute(far, 'head', other)  2.41 us
    pallas_call x1, Pallas kernels, prepare(): pl.pallas_call(prepare_kernel, out_shape=[jax.ShapeDtypeStruct((copies, q...  2.28 us
    ppermute x1, starting transfers between devices, body(): near = lax.ppermute(own, 'head', other)  1.92 us
  transfers between devices with their start and end apart: 4, of which 1 were waited for; matrix products, arithmetic and copies ran while one was open for 0% of the time, Pallas kernels for 0%

profile of v4, /device:TPU:448, one launch (start us, length us, event | category | flops | bytes accessed | tf_op | source)
XLA Modules:
  0.0 58.4 jit_solution(16573555605321098550)
XLA Ops:
  0.7 2.3 %prepare.1 = (bf16[16,96,128]{2,1,0:T(8,128)(2,1)}, bf16[2080,128]{1,0:T(8,128)(2,1)}, bf16[512,128]{1,0:T(8,128)(2,1)}) custom-call(s32[1,1]{1,0:T(1,128)} %bitcast.6.fill_ref, s32[512]{0:T(512)} %place_hbm.1, s32[4,128]{1,0:T(4,128)} %bitcast.9, bf16[32,384]{1,0:T(8,128)(2,1)} %q_hbm.1, bf16[1024,128]{1,0:T(8,128)(2,1)} %bitcast.7, ...), custom_call_target="tpu_custom_call" | custom-call | tf_op jit(solution)/shard_map/prepare/pallas_call | solution.py:250
  2.9 0.0 copy-start
  2.9 3.5 %collective-permute-start.1 = (bf16[2080,128]{1,0:T(8,128)(2,1)}, bf16[2080,128]{1,0:T(8,128)(2,1)S(1)}, u32[]{:S(2)}, u32[]{:S(2)}) collective-permute-start(bf16[2080,128]{1,0:T(8,128)(2,1)} %get-tuple-element.9.own_ref), channel_id=1, source_target_pairs={{0,2},{1,35},{2,0},{3,33},{4,6},{5,39},{6,4},{7,37},{8,10},{9,43},... | collective-permute-start | bytes 1597448 | tf_op jit(solution)/shard_map/ppermute | solution.py:317
  6.5 0.0 copy-start.1
  6.5 9.5 %all-to-all-start = ((bf16[16,96,128]{2,1,0:T(8,128)(2,1)}), bf16[16,96,128]{2,1,0:T(8,128)(2,1)S(1)}, u32[]{:S(2)}, u32[]{:S(2)}) async-start(bf16[16,96,128]{2,1,0:T(8,128)(2,1)} %get-tuple-element.8), calls=%async_computation | async-start | bytes 786432 | tf_op jit(solution)/shard_map/all_to_all | solution.py:316
  16.0 0.0 copy-done
  16.0 1.9 %collective-permute-start = (bf16[2080,128]{1,0:T(8,128)(2,1)S(1)}, bf16[2080,128]{1,0:T(8,128)(2,1)S(1)}, u32[]{:S(2)}, u32[]{:S(2)}) collective-permute-start(bf16[2080,128]{1,0:T(8,128)(2,1)S(1)} %copy-done), channel_id=1, source_target_pairs={{0,1},{1,0},{2,3},{3,2},{4,5},{5,4},{6,7},{7,6},{8,9},{9,8},{10,11... | collective-permute-start | bytes 1597448 | tf_op jit(solution)/shard_map/ppermute | solution.py:318
  18.0 0.0 collective-permute-done.1.far_ref
  18.0 2.4 %collective-permute-start.2 = (bf16[2080,128]{1,0:T(8,128)(2,1)S(1)}, bf16[2080,128]{1,0:T(8,128)(2,1)S(1)}, u32[]{:S(2)}, u32[]{:S(2)}) collective-permute-start(bf16[2080,128]{1,0:T(8,128)(2,1)S(1)} %collective-permute-done.1.far_ref), channel_id=1, source_target_pairs={{0,1},{1,0},{2,3},{3,2},{4,5},{5,4},{6,7},{7,6},{8,9},{9,8},{10,11... | collective-permute-start | bytes 1597448 | tf_op jit(solution)/shard_map/ppermute | solution.py:319
  20.4 0.0 collective-permute-done.near_ref
  20.4 10.9 %all-to-all-done.q_ref = bf16[16,96,128]{2,1,0:T(8,128)(2,1)S(1)} async-done(((bf16[16,96,128]{2,1,0:T(8,128)(2,1)}), bf16[16,96,128]{2,1,0:T(8,128)(2,1)S(1)}, u32[]{:S(2)}, u32[]{:S(2)}) %all-to-all-start) | async-done | bytes 393248 | tf_op jit(solution)/shard_map/all_to_all | solution.py:316
  31.3 0.0 collective-permute-done.2.diagonal_ref
  31.3 0.0 copy-done.1
  31.3 6.8 %attend.1 = bf16[16,112,128]{2,1,0:T(8,128)(2,1)S(1)} custom-call(bf16[16,96,128]{2,1,0:T(8,128)(2,1)S(1)} %all-to-all-done.q_ref, bf16[2080,128]{1,0:T(8,128)(2,1)S(1)} %copy-done, bf16[2080,128]{1,0:T(8,128)(2,1)S(1)} %collective-permute-done.near_ref, bf16[2080,128]{1,0:T(8,128)(2,1)S(1)} %collective-permute-done.1.far_ref, ...), custom_call_target="tpu_custom_call" | custom-call | flops 3221225472 | bytes 4194304 | tf_op jit(solution)/shard_map/attend/pallas_call | solution.py:276
  38.1 19.2 %all_to_all.10.part_ref = bf16[16,112,128]{2,1,0:T(8,128)(2,1)S(1)} all-to-all(bf16[16,112,128]{2,1,0:T(8,128)(2,1)S(1)} %attend.1), channel_id=1, replica_groups=mesh['ctx'=16,'head'=32] {'ctx'}, dimensions={0} | all-to-all | bytes 917504 | tf_op jit(solution)/shard_map/all_to_all | solution.py:321
  57.4 1.1 %combine.1 = bf16[32,384]{1,0:T(8,128)(2,1)} custom-call(bf16[16,112,128]{2,1,0:T(8,128)(2,1)S(1)} %all_to_all.10.part_ref), custom_call_target="tpu_custom_call" | custom-call | tf_op jit(solution)/shard_map/combine/pallas_call | solution.py:292
Async XLA Ops:
  2.9 13.1 %copy-start = (bf16[2080,128]{1,0:T(8,128)(2,1)S(1)}, bf16[2080,128]{1,0:T(8,128)(2,1)}, u32[]{:S(2)}) copy-start(bf16[2080,128]{1,0:T(8,128)(2,1)} %get-tuple-element.9.own_ref) | copy-start | bytes 1597444
  2.9 15.0 %collective-permute-start.1 = (bf16[2080,128]{1,0:T(8,128)(2,1)}, bf16[2080,128]{1,0:T(8,128)(2,1)S(1)}, u32[]{:S(2)}, u32[]{:S(2)}) collective-permute-start(bf16[2080,128]{1,0:T(8,128)(2,1)} %get-tuple-element.9.own_ref), channel_id=1, source_target_pairs={{0,2},{1,35},{2,0},{3,33},{4,6},{5,39},{6,4},{7,37},{8,10},{9,43},... | collective-permute-start | bytes 1597448 | tf_op jit(solution)/shard_map/ppermute | solution.py:317
  6.5 24.8 %copy-start.1 = (bf16[512,128]{1,0:T(8,128)(2,1)S(1)}, bf16[512,128]{1,0:T(8,128)(2,1)}, u32[]{:S(2)}) copy-start(bf16[512,128]{1,0:T(8,128)(2,1)} %get-tuple-element.10.bias_ref) | copy-start | bytes 393220
  6.5 24.8 %all-to-all-start = ((bf16[16,96,128]{2,1,0:T(8,128)(2,1)}), bf16[16,96,128]{2,1,0:T(8,128)(2,1)S(1)}, u32[]{:S(2)}, u32[]{:S(2)}) async-start(bf16[16,96,128]{2,1,0:T(8,128)(2,1)} %get-tuple-element.8), calls=%async_computation | async-start | bytes 786432 | tf_op jit(solution)/shard_map/all_to_all | solution.py:316
  16.0 4.4 %collective-permute-start = (bf16[2080,128]{1,0:T(8,128)(2,1)S(1)}, bf16[2080,128]{1,0:T(8,128)(2,1)S(1)}, u32[]{:S(2)}, u32[]{:S(2)}) collective-permute-start(bf16[2080,128]{1,0:T(8,128)(2,1)S(1)} %copy-done), channel_id=1, source_target_pairs={{0,1},{1,0},{2,3},{3,2},{4,5},{5,4},{6,7},{7,6},{8,9},{9,8},{10,11... | collective-permute-start | bytes 1597448 | tf_op jit(solution)/shard_map/ppermute | solution.py:318
  18.0 13.3 %collective-permute-start.2 = (bf16[2080,128]{1,0:T(8,128)(2,1)S(1)}, bf16[2080,128]{1,0:T(8,128)(2,1)S(1)}, u32[]{:S(2)}, u32[]{:S(2)}) collective-permute-start(bf16[2080,128]{1,0:T(8,128)(2,1)S(1)} %collective-permute-done.1.far_ref), channel_id=1, source_target_pairs={{0,1},{1,0},{2,3},{3,2},{4,5},{5,4},{6,7},{7,6},{8,9},{9,8},{10,11... | collective-permute-start | bytes 1597448 | tf_op jit(solution)/shard_map/ppermute | solution.py:319
